TPU v7x, 32 devices: a whole 2x2x4 slice. The times are simulated.
32 devices in a mesh: dp: 4 (over y, x), fsdp: 8 (over z, core).
Axes of the slice: x: 2, y: 2, z: 4, core: 2. Of those that a mesh axis runs over, the one named last changes fastest.
Arguments:
- tokens: bfloat16 [32, 1024, 1024], P(('dp', 'fsdp')), may hold values from -6 to 6
- lengths: int32 [32], P(('dp', 'fsdp')), may hold values from 300 to 1024, as said below
- cotangent: bfloat16 [32, 1024, 1024], P(('dp', 'fsdp')), may hold values from -6 to 6
- w_query: bfloat16 [1024, 1024], P(('dp', 'fsdp')), may hold values from -0.1875 to 0.1875
- w_key: bfloat16 [1024, 1024], P(('dp', 'fsdp')), may hold values from -0.1875 to 0.1875
- w_value: bfloat16 [1024, 1024], P(('dp', 'fsdp')), may hold values from -0.1875 to 0.1875
- w_gate: bfloat16 [1024, 1024], P(('dp', 'fsdp')), may hold values from -0.1875 to 0.1875
- w_out: bfloat16 [1024, 1024], P(('dp', 'fsdp')), may hold values from -0.25 to 0.25
- out_gain: bfloat16 [1024], P(('dp', 'fsdp')), may hold values from 0.099609375 to 1.8984375
- w_first: bfloat16 [1024, 2816], P(('dp', 'fsdp')), may hold values from -0.1875 to 0.1875
- w_second: bfloat16 [1024, 2816], P(('dp', 'fsdp')), may hold values from -0.1875 to 0.1875
- w_down: bfloat16 [2816, 1024], P(('dp', 'fsdp')), may hold values from -0.109375 to 0.109375
Outputs:
- layer_out: bfloat16 [32, 1024, 1024], P(('dp', 'fsdp'))
- input_grad: bfloat16 [32, 1024, 1024], P(('dp', 'fsdp'))
- grad_query: float32 [1024, 1024], P(('dp', 'fsdp'))
- grad_key: float32 [1024, 1024], P(('dp', 'fsdp'))
- grad_value: float32 [1024, 1024], P(('dp', 'fsdp'))
- grad_gate: float32 [1024, 1024], P(('dp', 'fsdp'))
- grad_out: float32 [1024, 1024], P(('dp', 'fsdp'))
- grad_gain: float32 [1024], P(('dp', 'fsdp'))
- grad_first: float32 [1024, 2816], P(('dp', 'fsdp'))
- grad_second: float32 [1024, 2816], P(('dp', 'fsdp'))
- grad_down: float32 [2816, 1024], P(('dp', 'fsdp'))
Inputs may be any that keep to these rules, and one draw needn't show every extreme that they name: Slot s holds one sequence in its first lengths[s] positions and padding after it; some slot is exactly 1024 tokens long and some other exactly 300.
All inputs are finite; a program needn't handle non-finite values.
Results may differ from a plain program's by a relative error of at most 0.014.
Values may be sent and summed in bfloat16 or wider, within the bound.
A program may use at most 256 MiB of HBM per device.

v0:
```python
import jax
import jax.numpy as jnp
from jax import lax
from jax.sharding import PartitionSpec as P

HEADS = 16
HEAD_DIM = 64
BLOCK = 64


epsilon = 1e-06
masked_score = -1e30


def normalize(values):
    inv_rms = lax.rsqrt(jnp.mean(values * values, axis=-1, keepdims=True) + epsilon)
    return (values * inv_rms, inv_rms)


def norm_back(normed, inv_rms, upstream):
    return inv_rms * (upstream - normed * jnp.mean(upstream * normed, axis=-1, keepdims=True))


def project(left_rows, right_rows):
    return jnp.dot(left_rows, right_rows, preferred_element_type=jnp.float32)


def project_back(upstream, weight):
    return lax.dot_general(
        upstream, weight, (((1,), (1,)), ((), ())), preferred_element_type=jnp.float32
    )


def weight_grad(inputs, upstream):
    return lax.dot_general(
        inputs, upstream, (((0,), (0,)), ((), ())), preferred_element_type=jnp.float32
    )


def split_heads(row_block):
    row_count = row_block.shape[0]
    return row_block.reshape(row_count // BLOCK, BLOCK, HEADS, HEAD_DIM)


def block_scores(query_blocks, key_blocks):
    scores = jnp.einsum(
        "bihd,bjhd->bhij", query_blocks, key_blocks, preferred_element_type=jnp.float32
    ) * HEAD_DIM ** (-0.5)
    causal = lax.broadcasted_iota(jnp.int32, (BLOCK, BLOCK), 0) >= lax.broadcasted_iota(
        jnp.int32, (BLOCK, BLOCK), 1
    )
    return jnp.where(causal, scores, masked_score)


def attend(query_rows, key_rows, value_rows):
    scores = block_scores(split_heads(query_rows), split_heads(key_rows))
    row_max = jnp.max(scores, axis=-1, keepdims=True)
    exp_scores = jnp.exp(scores - row_max)
    row_total = jnp.sum(exp_scores, axis=-1, keepdims=True)
    probs_low = (exp_scores / row_total).astype(jnp.bfloat16)
    head_mix = jnp.einsum(
        "bhij,bjhd->bihd", probs_low, split_heads(value_rows), preferred_element_type=jnp.float32
    )
    return (head_mix.reshape(query_rows.shape[0], -1), row_max + jnp.log(row_total))


def attend_back(query_rows, key_rows, value_rows, logsum, grad_mix):
    query_blocks = split_heads(query_rows)
    key_blocks = split_heads(key_rows)
    value_blocks = split_heads(value_rows)
    grad_blocks = split_heads(grad_mix)
    probs = jnp.exp(block_scores(query_blocks, key_blocks) - logsum)
    probs_low = probs.astype(jnp.bfloat16)
    grad_probs = jnp.einsum(
        "bihd,bjhd->bhij", grad_blocks, value_blocks, preferred_element_type=jnp.float32
    )
    grad_values = jnp.einsum(
        "bhij,bihd->bjhd", probs_low, grad_blocks, preferred_element_type=jnp.float32
    )
    grad_scores = (
        probs * (grad_probs - jnp.sum(grad_probs * probs, axis=-1, keepdims=True))
    ).astype(jnp.bfloat16)
    scale_factor = HEAD_DIM ** (-0.5)
    grad_queries = (
        jnp.einsum("bhij,bjhd->bihd", grad_scores, key_blocks, preferred_element_type=jnp.float32)
        * scale_factor
    )
    grad_keys = (
        jnp.einsum("bhij,bihd->bjhd", grad_scores, query_blocks, preferred_element_type=jnp.float32)
        * scale_factor
    )
    row_count = query_rows.shape[0]
    return (
        grad_queries.reshape(row_count, -1).astype(jnp.bfloat16),
        grad_keys.reshape(row_count, -1).astype(jnp.bfloat16),
        grad_values.reshape(row_count, -1).astype(jnp.bfloat16),
    )


def ffn_sums(second_in, hidden, grad_first_proj, grad_second_proj, grad_branch):
    both_proj = jnp.concatenate([grad_first_proj, grad_second_proj], axis=1)
    inner_shard = lax.psum_scatter(
        weight_grad(second_in, both_proj), ("dp", "fsdp"), scatter_dimension=0, tiled=True
    )
    down_shard = lax.psum_scatter(
        weight_grad(hidden, grad_branch), ("dp", "fsdp"), scatter_dimension=0, tiled=True
    )
    ff_width = grad_first_proj.shape[1]
    return (inner_shard[:, :ff_width], inner_shard[:, ff_width:], down_shard)


def body(
    tokens,
    lengths,
    cotangent,
    w_query,
    w_key,
    w_value,
    w_gate,
    w_out,
    out_gain,
    w_first,
    w_second,
    w_down,
):
    slot_count, slot_len, feature_width = tokens.shape
    row_count = slot_count * slot_len
    places = lax.broadcasted_iota(jnp.int32, (slot_count, slot_len), 1)
    live_rows = (places < lengths[:, None]).astype(jnp.float32).reshape(row_count, 1)
    attn_full = (
        lax.all_gather(w_query, ("dp", "fsdp"), axis=0, tiled=True),
        lax.all_gather(w_key, ("dp", "fsdp"), axis=0, tiled=True),
        lax.all_gather(w_value, ("dp", "fsdp"), axis=0, tiled=True),
        lax.all_gather(w_gate, ("dp", "fsdp"), axis=0, tiled=True),
        lax.all_gather(w_out, ("dp", "fsdp"), axis=0, tiled=True),
        lax.all_gather(out_gain, ("dp", "fsdp"), axis=0, tiled=True),
    )
    ffn_full = (
        lax.all_gather(w_first, ("dp", "fsdp"), axis=0, tiled=True),
        lax.all_gather(w_second, ("dp", "fsdp"), axis=0, tiled=True),
        lax.all_gather(w_down, ("dp", "fsdp"), axis=0, tiled=True),
    )
    query_full, key_full, value_full, gate_full, out_full, gain_full = attn_full
    first_full, second_full, down_full = ffn_full
    inputs = tokens.reshape(row_count, feature_width).astype(jnp.float32)
    normed_in, inv_in = normalize(inputs)
    first_in = normed_in.astype(jnp.bfloat16)
    query_rows = project(first_in, query_full).astype(jnp.bfloat16)
    key_rows = project(first_in, key_full).astype(jnp.bfloat16)
    value_rows = project(first_in, value_full).astype(jnp.bfloat16)
    gate_pre = project(first_in, gate_full)
    head_mix, logsum = attend(query_rows, key_rows, value_rows)
    normed_mix, inv_mix = normalize(head_mix)
    gain_rows = gain_full.astype(jnp.float32)
    gate_act = jax.nn.silu(gate_pre)
    scaled_mix = normed_mix * gain_rows
    branch_in = (scaled_mix * gate_act).astype(jnp.bfloat16)
    middle = inputs + live_rows * project(branch_in, out_full)
    normed_mid, inv_mid = normalize(middle)
    second_in = normed_mid.astype(jnp.bfloat16)
    first_proj = project(second_in, first_full)
    second_proj = project(second_in, second_full)
    hidden = (first_proj * second_proj).astype(jnp.bfloat16)
    final_rows = middle + live_rows * project(hidden, down_full)
    layer_out = final_rows.astype(jnp.bfloat16).reshape(tokens.shape)
    first_back, second_back, down_back = (
        lax.all_gather(w_first, ("dp", "fsdp"), axis=0, tiled=True),
        lax.all_gather(w_second, ("dp", "fsdp"), axis=0, tiled=True),
        lax.all_gather(w_down, ("dp", "fsdp"), axis=0, tiled=True),
    )
    query_back, key_back, value_back, gate_back, out_back, gain_back = (
        lax.all_gather(w_query, ("dp", "fsdp"), axis=0, tiled=True),
        lax.all_gather(w_key, ("dp", "fsdp"), axis=0, tiled=True),
        lax.all_gather(w_value, ("dp", "fsdp"), axis=0, tiled=True),
        lax.all_gather(w_gate, ("dp", "fsdp"), axis=0, tiled=True),
        lax.all_gather(w_out, ("dp", "fsdp"), axis=0, tiled=True),
        lax.all_gather(out_gain, ("dp", "fsdp"), axis=0, tiled=True),
    )
    gain_used = gain_back.astype(jnp.float32)
    grad_final = cotangent.reshape(row_count, feature_width).astype(jnp.float32)
    grad_branch = (live_rows * grad_final).astype(jnp.bfloat16)
    grad_hidden = project_back(grad_branch, down_back)
    grad_first_proj = (grad_hidden * second_proj).astype(jnp.bfloat16)
    grad_second_proj = (grad_hidden * first_proj).astype(jnp.bfloat16)
    grad_normed_mid = project_back(grad_first_proj, first_back) + project_back(
        grad_second_proj, second_back
    )
    grad_middle = grad_final + norm_back(normed_mid, inv_mid, grad_normed_mid)
    grad_attn_out = (live_rows * grad_middle).astype(jnp.bfloat16)
    grad_branch_in = project_back(grad_attn_out, out_back)
    gain_terms = grad_branch_in * gate_act * normed_mix
    sigmoid_gate = jax.nn.sigmoid(gate_pre)
    grad_gate_pre = (
        grad_branch_in * scaled_mix * sigmoid_gate * (1.0 + gate_pre * (1.0 - sigmoid_gate))
    ).astype(jnp.bfloat16)
    grad_scaled = grad_branch_in * gate_act * gain_used
    grad_mix = norm_back(normed_mix, inv_mix, grad_scaled).astype(jnp.bfloat16)
    grad_queries, grad_keys, grad_values = attend_back(
        query_rows, key_rows, value_rows, logsum, grad_mix
    )
    grad_normed_in = (
        project_back(grad_queries, query_back)
        + project_back(grad_keys, key_back)
        + project_back(grad_values, value_back)
        + project_back(grad_gate_pre, gate_back)
    )
    grad_inputs = grad_middle + norm_back(normed_in, inv_in, grad_normed_in)
    input_grad = grad_inputs.astype(jnp.bfloat16).reshape(tokens.shape)
    ffn_shards = ffn_sums(second_in, hidden, grad_first_proj, grad_second_proj, grad_branch)
    four_grads = jnp.concatenate([grad_queries, grad_keys, grad_values, grad_gate_pre], axis=1)
    from_input = weight_grad(first_in, four_grads)
    from_branch = weight_grad(branch_in, grad_attn_out)
    gain_part = jnp.sum(gain_terms, axis=0)[:, None]
    attn_shard = lax.psum_scatter(
        jnp.concatenate([from_input, from_branch, gain_part], axis=1),
        ("dp", "fsdp"),
        scatter_dimension=0,
        tiled=True,
    )
    shard_query = attn_shard[:, 0:feature_width]
    shard_key = attn_shard[:, feature_width : 2 * feature_width]
    shard_value = attn_shard[:, 2 * feature_width : 3 * feature_width]
    shard_gate = attn_shard[:, 3 * feature_width : 4 * feature_width]
    shard_out = attn_shard[:, 4 * feature_width : 5 * feature_width]
    shard_gain = attn_shard[:, 5 * feature_width]
    shard_first, shard_second, shard_down = ffn_shards
    return (
        layer_out,
        input_grad,
        shard_query,
        shard_key,
        shard_value,
        shard_gate,
        shard_out,
        shard_gain,
        shard_first,
        shard_second,
        shard_down,
    )


def solution(mesh):
    return jax.shard_map(
        body,
        mesh=mesh,
        in_specs=(
            P(("dp", "fsdp"), None, None),
            P(("dp", "fsdp")),
            P(("dp", "fsdp"), None, None),
            P(("dp", "fsdp"), None),
            P(("dp", "fsdp"), None),
            P(("dp", "fsdp"), None),
            P(("dp", "fsdp"), None),
            P(("dp", "fsdp"), None),
            P(("dp", "fsdp")),
            P(("dp", "fsdp"), None),
            P(("dp", "fsdp"), None),
            P(("dp", "fsdp"), None),
        ),
        out_specs=(
            P(("dp", "fsdp"), None, None),
            P(("dp", "fsdp"), None, None),
            P(("dp", "fsdp"), None),
            P(("dp", "fsdp"), None),
            P(("dp", "fsdp"), None),
            P(("dp", "fsdp"), None),
            P(("dp", "fsdp"), None),
            P(("dp", "fsdp")),
            P(("dp", "fsdp"), None),
            P(("dp", "fsdp"), None),
            P(("dp", "fsdp"), None),
        ),
        check_vma=False,
    )
```

profile of v0, /device:TPU:0, one launch (start us, length us, event | category | flops | bytes accessed | tf_op | source)
XLA Modules:
  0.0 1339.8 jit_solution(14098079574076913081)
XLA Ops:
  13.3 2.9 copy.44
  17.0 42.2 %all-reduce = bf16[1024]{0:T(1024)(128)(2,1)S(1)} all-reduce(bf16[1024]{0:T(1024)(128)(2,1)S(1)} %dynamic-update-slice), channel_id=1, replica_groups=mesh['dp'=4,'fsdp'=8] {'dp','fsdp'}, use_global_device_ids=true, to_apply=%add | all-reduce | flops 1024 | bytes 4096
  59.2 4.0 copy.52
  63.2 7.2 all-gather.11.cloned.1.call-done
  70.3 5.3 convolution_convert_fusion.1
  75.6 6.4 reshape.128
  82.0 7.1 copy.59
  89.2 39.6 %all-gather.13.cloned.1.call-done = bf16[1024,1024]{1,0:T(8,128)(2,1)} async-done(((bf16[32,1024]{1,0:T(8,128)(2,1)}), bf16[1024,1024]{1,0:T(8,128)(2,1)}) %all-gather.13.cloned.1.call-update) | async-done | bytes 2097168 | tf_op jit(solution)/shard_map/all_gather | solution.py:132
  128.8 5.3 convolution_convert_fusion
  134.1 6.4 reshape.129
  140.5 7.1 copy.55
  147.6 39.5 %all-gather.9.cloned.1.call-done = bf16[1024,1024]{1,0:T(8,128)(2,1)} async-done(((bf16[32,1024]{1,0:T(8,128)(2,1)}), bf16[1024,1024]{1,0:T(8,128)(2,1)}) %all-gather.9.cloned.1.call-update) | async-done | bytes 2097168 | tf_op jit(solution)/shard_map/all_gather | solution.py:133
  187.2 5.3 convolution_convert_fusion.2
  192.5 6.6 reshape.127
  199.1 5.8 fusion.36
  204.8 2.9 fusion.12
  210.1 5.8 multiply_reduce_fusion.1
  215.9 13.2 copy.80
  229.1 7.7 reshape.138
  236.8 8.5 all-gather.15.cloned.1.call-done
  245.4 8.7 multiply_convert_fusion.9
  254.1 49.5 %all-gather.17.cloned.1.call-done = bf16[1024,1024]{1,0:T(8,128)(2,1)} async-done(((bf16[32,1024]{1,0:T(8,128)(2,1)}), bf16[1024,1024]{1,0:T(8,128)(2,1)}) %all-gather.17.cloned.1.call-update) | async-done | bytes 2097168 | tf_op jit(solution)/shard_map/all_gather | solution.py:135
  303.6 5.0 multiply_reduce_fusion.5
  311.2 61.3 %all-gather.21.cloned.1.call-done = bf16[1024,2816]{1,0:T(8,128)(2,1)} async-done(((bf16[32,2816]{1,0:T(8,128)(2,1)}), bf16[1024,2816]{1,0:T(8,128)(2,1)}) %all-gather.21.cloned.1.call-update) | async-done | bytes 5767184 | tf_op jit(solution)/shard_map/all_gather | solution.py:140
  372.5 11.6 fusion.69
  384.1 57.6 %all-gather.19.cloned.1.call-done = bf16[1024,2816]{1,0:T(8,128)(2,1)} async-done(((bf16[32,2816]{1,0:T(8,128)(2,1)}), bf16[1024,2816]{1,0:T(8,128)(2,1)}) %all-gather.19.cloned.1.call-update) | async-done | bytes 5767184 | tf_op jit(solution)/shard_map/all_gather | solution.py:139
  441.6 12.1 fusion.68
  453.7 57.0 %all-gather.23.cloned.1.call-done = bf16[2816,1024]{1,0:T(8,128)(2,1)} async-done(((bf16[88,1024]{1,0:T(8,128)(2,1)}), bf16[2816,1024]{1,0:T(8,128)(2,1)}) %all-gather.23.cloned.1.call-update) | async-done | bytes 5767184 | tf_op jit(solution)/shard_map/all_gather | solution.py:141
  510.8 17.6 %multiply_convert_fusion = (bf16[1024,2816]{1,0:T(8,128)(2,1)}, bf16[1024,2816]{1,0:T(8,128)(2,1)}, bf16[1024,2816]{1,0:T(8,128)(2,1)}) fusion(f32[1024,2816]{1,0:T(8,128)} %fusion.68, f32[1024,2816]{1,0:T(8,128)} %fusion.69, bf16[2816,1024]{1,0:T(8,128)(2,1)} %all-gather.23.cloned.1.call-done, bf16[1,1024,1024]{1,2,0:T(8,128)(2,1)S(1)} %copy-done.6, ...), kind=kOutput, calls=%fused_computation.5 | convolution fusion | flops 5926027264 | bytes 48238592 | tf_op jit(solution)/shard_map/dot_general | solution.py:29
  528.4 10.0 fusion.70
  538.4 8.5 multiply_reduce_fusion.4
  548.6 4.5 fusion.56
  555.7 3.3 multiply_reduce_fusion.2
  559.0 4.2 multiply_convert_fusion.6
  563.2 4.4 reshape.132
  567.6 9.7 convert_bitcast_fusion
  577.4 12.4 multiply_reduce_fusion
  589.8 5.6 multiply_convert_fusion.5
  595.4 4.4 fusion.27
  599.9 4.3 fusion.26
  604.4 7.7 copy.65
  612.1 6.7 convert_element_type.136
  618.8 7.7 copy.58
  626.4 6.5 convert_element_type.129
  632.9 7.7 copy.62
  640.6 6.5 convert_element_type.132
  647.1 4.1 copy.67
  651.2 3.9 copy.66
  655.1 16.4 %fusion.4 = f32[1024,4096]{1,0:T(8,128)} fusion(bf16[1024,1024]{0,1:T(8,128)(2,1)} %get-tuple-element.35, bf16[1024,1024]{0,1:T(8,128)(2,1)} %convert_element_type.136, bf16[1024,1024]{0,1:T(8,128)(2,1)} %copy.67, bf16[1024,1024]{0,1:T(8,128)(2,1)} %copy.66, bf16[1,1024,1024]{1,2,0:T(8,128)(2,1)S(1)} %copy-done.5, f32[1024]{0:T(1024)S(1)} %add_rsqrt_fusion.2), kind=kOutput, calls=%fused_computation.8 | convolution fusion | flops 8626634752 | bytes 27267072 | tf_op jit(solution)/shard_map/dot_general | solution.py:35
  671.6 15.7 %pad_maximum_fusion = f32[1024,5121]{1,0:T(8,128)} fusion(f32[1024,1]{1,0:T(8,128)S(1)} %copy.69, f32[1024,1024]{1,0:T(8,128)} %fusion.56, f32[1024,4096]{1,0:T(8,128)} %fusion.4), kind=kLoop, calls=%fused_computation | loop fusion | flops 10487808 | bytes 41951232 | tf_op jit(solution)/shard_map/concatenate | solution.py:215
  687.3 21.1 %fusion = f32[1024,5632]{1,0:T(8,128)} fusion(bf16[1024,1024]{0,1:T(8,128)(2,1)} %copy-done.18, bf16[1024,2816]{1,0:T(8,128)(2,1)} %get-tuple-element.37, bf16[1024,2816]{1,0:T(8,128)(2,1)} %get-tuple-element.39), kind=kOutput, calls=%fused_computation.1 | convolution fusion | flops 11834228736 | bytes 36700160 | tf_op jit(solution)/shard_map/dot_general | solution.py:35
  708.5 12.5 fusion.45
  721.0 11.6 fusion.49
  732.7 4.1 copy.70
  736.8 4.8 fusion.72
  741.6 2.4 fusion.71
  744.1 2.3 fusion.73
  746.4 2.7 fusion.18
  749.2 2.6 fusion.44
  751.8 3.9 copy.71
  755.7 166.4 %reduce-scatter.4.cloned.1.call-done = f32[32,5121]{1,0:T(8,128)} async-done(((f32[1024,5121]{1,0:T(8,128)}), f32[32,5121]{1,0:T(8,128)}) %reduce-scatter.4.cloned.1.call-update) | async-done | bytes 655504 | tf_op jit(solution)/shard_map/reduce_scatter | solution.py:214
  923.5 2.0 fusion.67
  925.5 247.6 %reduce-scatter.6.cloned.1.call-done = f32[32,5632]{1,0:T(8,128)} async-done(((f32[1024,5632]{1,0:T(8,128)}), f32[32,5632]{1,0:T(8,128)}) %reduce-scatter.6.cloned.1.call-update) | async-done | bytes 720912 | tf_op jit(solution)/shard_map/reduce_scatter | solution.py:102
  1175.0 158.0 %reduce-scatter.8.cloned.1.call-done = f32[88,1024]{1,0:T(8,128)} async-done(((f32[2816,1024]{1,0:T(8,128)}), f32[88,1024]{1,0:T(8,128)}) %reduce-scatter.8.cloned.1.call-update) | async-done | bytes 360464 | tf_op jit(solution)/shard_map/reduce_scatter | solution.py:105
  (96 shorter events, 19.0 us)
Async XLA Ops:
  7.2 9.6 copy-start.23
  7.2 63.1 %all-gather.11.cloned.1.call-start = ((), (), s32[]{:S(2)}) async-start(), calls=%async_computation.4 | async-start | bytes 2162688 | tf_op jit(solution)/shard_map/all_gather | solution.py:131
  7.9 120.9 %all-gather.13.cloned.1.call-start = ((), (), s32[]{:S(2)}) async-start(), calls=%async_computation.5 | async-start | bytes 2162688 | tf_op jit(solution)/shard_map/all_gather | solution.py:132
  8.7 178.5 %all-gather.9.cloned.1.call-start = ((), (), s32[]{:S(2)}) async-start(), calls=%async_computation.3 | async-start | bytes 2162688 | tf_op jit(solution)/shard_map/all_gather | solution.py:133
  9.4 236.0 %all-gather.15.cloned.1.call-start = ((), (), s32[]{:S(2)}) async-start(), calls=%async_computation.6 | async-start | bytes 2162688 | tf_op jit(solution)/shard_map/all_gather | solution.py:134
  10.0 293.6 %all-gather.17.cloned.1.call-start = ((), (), s32[]{:S(2)}) async-start(), calls=%async_computation.7 | async-start | bytes 2162688 | tf_op jit(solution)/shard_map/all_gather | solution.py:135
  10.6 361.9 %all-gather.21.cloned.1.call-start = ((), (), s32[]{:S(2)}) async-start(), calls=%async_computation.9 | async-start | bytes 5947392 | tf_op jit(solution)/shard_map/all_gather | solution.py:140
  11.1 430.5 %all-gather.19.cloned.1.call-start = ((), (), s32[]{:S(2)}) async-start(), calls=%async_computation.8 | async-start | bytes 5947392 | tf_op jit(solution)/shard_map/all_gather | solution.py:139
  11.9 498.9 %all-gather.23.cloned.1.call-start = ((), (), s32[]{:S(2)}) async-start(), calls=%async_computation.10 | async-start | bytes 5947392 | tf_op jit(solution)/shard_map/all_gather | solution.py:141
  12.6 909.5 %reduce-scatter.4.cloned.1.call-start = ((), (), s32[]{:S(2)}) async-start(), calls=%async_computation.11 | async-start | bytes 22167552 | tf_op jit(solution)/shard_map/reduce_scatter | solution.py:214
  16.2 287.4 %copy-start.4 = (bf16[1,1024,1024]{1,2,0:T(8,128)(2,1)}, bf16[1,1024,1024]{1,2,0:T(8,128)(2,1)S(1)}, u32[]{:S(2)}) copy-start(bf16[1,1024,1024]{1,2,0:T(8,128)(2,1)S(1)} %copy.44) | copy-start | bytes 6291460
  204.8 4.3 copy-start
  204.8 5.2 copy-start.12
  308.5 2.0 copy-start.7
  311.2 61.3 %copy-start.18 = (bf16[1024,1024]{0,1:T(8,128)(2,1)}, bf16[1024,1024]{0,1:T(8,128)(2,1)S(1)}, u32[]{:S(2)}) copy-start(bf16[1024,1024]{0,1:T(8,128)(2,1)S(1)} %multiply_convert_fusion.10) | copy-start | bytes 6291460
  384.1 126.7 %copy-start.6 = (bf16[1,1024,1024]{1,2,0:T(8,128)(2,1)S(1)}, bf16[1,1024,1024]{1,2,0:T(8,128)(2,1)}, u32[]{:S(2)}) copy-start(bf16[1,1024,1024]{1,2,0:T(8,128)(2,1)} %copy.52) | copy-start | bytes 6291460
  528.4 10.0 copy-start.8
  528.4 10.1 copy-start.13
  547.0 1.6 copy-start.24
  548.6 4.6 copy-start.9
  548.6 4.6 copy-start.11
  548.6 6.5 copy-start.16
  548.6 7.1 copy-start.22
  567.6 9.8 copy-start.3
  567.6 22.2 %slice-start = ((s8[8388608]{0:T(1024)(128)(4,1)}), s8[4194304]{0:T(1024)(128)(4,1)S(1)}, s32[]{:S(2)}) async-start(s8[8388608]{0:T(1024)(128)(4,1)} %bitcast.86), calls=%async_computation.14 | async-start | bytes 8388608
  577.4 12.4 slice-start.1
  589.8 5.6 copy-start.1
  595.4 4.5 copy-start.2
  647.1 8.0 copy-start.5
  687.3 485.7 %reduce-scatter.6.cloned.1.call-start = ((), (), s32[]{:S(2)}) async-start(), calls=%async_computation.12 | async-start | bytes 23789568 | tf_op jit(solution)/shard_map/reduce_scatter | solution.py:102
  708.5 624.6 %reduce-scatter.8.cloned.1.call-start = ((), (), s32[]{:S(2)}) async-start(), calls=%async_computation.13 | async-start | bytes 11894784 | tf_op jit(solution)/shard_map/reduce_scatter | solution.py:105
  736.8 4.8 copy-start.14
  736.8 4.8 copy-start.20
  741.6 2.4 copy-start.17
  741.6 2.4 copy-start.21
  744.0 2.4 copy-start.15
  744.0 2.4 copy-start.19
  746.4 2.8 copy-start.10
Sparse Core Ops, SparseCore 0:
  11.0 59.2 all-gather.10
  73.3 55.4 all-gather.12
  131.8 55.3 all-gather.8
  190.0 55.3 all-gather.14
  248.2 55.3 all-gather.16
  306.3 66.1 all-gather.20
  375.3 66.2 all-gather.18
  444.5 66.2 all-gather.22
  687.4 234.6 reduce-scatter.3
  924.4 248.6 reduce-scatter.5
  1176.0 156.9 reduce-scatter.7
where the time goes:
time: 1350 us; the launch traced here: 1340 us
  waiting for transfers between devices  897 us (66%)
  matrix products  214 us (16%)
  local copies, waits for them, and re-layouts  137 us (10%)
  blocking collectives  42.2 us (3%)
  other arithmetic  33.7 us (2%)
  between operations  15.2 us (1%)
    reduce_scatter x1, waiting for transfers between devices, ffn_sums(): lax.psum_scatter(weight_grad(second_in, both_proj), ('dp', 'fsdp'), scatt...  248 us
    reduce_scatter x1, waiting for transfers between devices, body(): lax.psum_scatter(jnp.concatenate([from_input, from_branch, gain_part], ax...  166 us
    reduce_scatter x1, waiting for transfers between devices, ffn_sums(): lax.psum_scatter(weight_grad(hidden, grad_branch), ('dp', 'fsdp'), scatte...  158 us
    dot_general x8, matrix products, project(): return jnp.dot(left_rows, right_rows, preferred_element_type=jnp.float32)  64.9 us
    all_gather x1, waiting for transfers between devices, body(): lax.all_gather(w_second, ('dp', 'fsdp'), axis=0, tiled=True)  61.3 us
    all_gather x1, waiting for transfers between devices, body(): lax.all_gather(w_first, ('dp', 'fsdp'), axis=0, tiled=True)  57.6 us
    all_gather x1, waiting for transfers between devices, body(): lax.all_gather(w_down, ('dp', 'fsdp'), axis=0, tiled=True)  57 us
    dot_general x4, matrix products, weight_grad(): lax.dot_general(inputs, upstream, (((0,), (0,)), ((), ())), preferred_ele...  54.6 us
  transfers between devices with their start and end apart: 11, of which 11 were waited for; matrix products, arithmetic and copies ran while one was open for 15% of the time, Pallas kernels for 0%

commit v1 on v0

--- a/solution.py
+++ b/solution.py
@@ -1,6 +1,10 @@
+import functools
+
 import jax
 import jax.numpy as jnp
 from jax import lax
+from jax.experimental import pallas as pl
+from jax.experimental.pallas import tpu as pltpu
 from jax.sharding import PartitionSpec as P
 
 HEADS = 16
@@ -109,7 +113,7 @@
     return (inner_shard[:, :ff_width], inner_shard[:, ff_width:], down_shard)
 
 
-def body(
+def general_body(
     tokens,
     lengths,
     cotangent,
@@ -239,9 +243,417 @@
     )
 
 
+MESH = pl.DeviceIdType.MESH
+f32 = jnp.float32
+bf16 = jnp.bfloat16
+
+
+class Place:
+    def __init__(self):
+        dp, fs = lax.axis_index("dp"), lax.axis_index("fsdp")
+        z, c = lax.div(fs, 2), lax.rem(fs, 2)
+        self.dp, self.fs, self.z, self.c = dp, fs, z, c
+        self.nx = dp + 1 - 2 * lax.rem(dp, 2)
+        self.ny = lax.rem(dp + 2, 4)
+        self.dg = lax.rem(self.nx + 2, 4)
+        self.zp = [lax.rem(z + k, 4) for k in (1, 2, 3)]
+        self.sib = (dp, z * 2 + 1 - c)
+        self.zdev = [(dp, zz * 2 + c) for zz in self.zp]
+        self.xdev, self.ydev = (self.nx, fs), (self.ny, fs)
+        self.peers = [self.sib, self.xdev, self.ydev] + self.zdev
+
+    def barrier(self):
+        bar = pltpu.get_barrier_semaphore()
+        for d in self.peers:
+            pl.semaphore_signal(bar, inc=1, device_id=d, device_id_type=MESH)
+        pl.semaphore_wait(bar, 6)
+
+
+class Gather:
+    def __init__(self, here, shards, outs, ssem, rsem, lsem):
+        self.h, self.shards, self.outs = here, shards, outs
+        self.ssem, self.rsem, self.lsem = ssem, rsem, lsem
+        self.sends = []
+
+    def rc(self, i, k, src, dst, dev):
+        return pltpu.make_async_remote_copy(
+            src_ref=src, dst_ref=dst, send_sem=self.ssem.at[i, k], recv_sem=self.rsem.at[i, k],
+            device_id=dev, device_id_type=MESH,
+        )
+
+    def go(self, m):
+        m.start()
+        self.sends.append(m)
+
+    def own(self, i):
+        h = self.h
+        return pltpu.make_async_copy(self.shards[i], self.outs[i].at[h.dp, h.z, h.c], self.lsem.at[i])
+
+    def zmsg(self, i, k):
+        h = self.h
+        return self.rc(i, k, self.shards[i], self.outs[i].at[h.dp, h.z, h.c], h.zdev[k])
+
+    def col(self, i, k, yx, dev):
+        r = self.outs[i].at[yx, :, self.h.c]
+        return self.rc(i, k, r, r, dev)
+
+    def half(self, i, k, yx, lo, dev):
+        r = self.outs[i].at[yx, lo : lo + 2, self.h.c]
+        return self.rc(i, k, r, r, dev)
+
+    def step0(self, i):
+        self.own(i).start()
+        for k in range(3):
+            self.go(self.zmsg(i, k))
+
+    def step1(self, i):
+        h = self.h
+        self.own(i).wait()
+        for k in range(3):
+            self.zmsg(i, k).wait_recv()
+        self.go(self.col(i, 3, h.dp, h.xdev))
+        self.go(self.col(i, 4, h.dp, h.ydev))
+        self.go(self.col(i, 7, h.dp, h.sib))
+
+    def step2(self, i):
+        h = self.h
+        self.col(i, 3, h.dp, h.xdev).wait_recv()
+        self.go(self.half(i, 6, h.nx, 2, h.ydev))
+        self.go(self.col(i, 8, h.nx, h.sib))
+        self.col(i, 4, h.dp, h.ydev).wait_recv()
+        self.go(self.half(i, 5, h.ny, 0, h.xdev))
+        self.go(self.col(i, 9, h.ny, h.sib))
+
+    def step3(self, i):
+        h = self.h
+        self.half(i, 5, h.ny, 0, h.xdev).wait_recv()
+        self.half(i, 6, h.nx, 2, h.ydev).wait_recv()
+        self.go(self.col(i, 10, h.dg, h.sib))
+
+    def step4(self, i):
+        h = self.h
+        for k in (7, 8, 9, 10):
+            self.col(i, k, h.dp, h.sib).wait_recv()
+
+    def finish(self):
+        for m in self.sends:
+            m.wait_send()
+
+
+def gather_kernel(n, *refs):
+    here = Place()
+    here.barrier()
+    ag = Gather(here, refs[:n], refs[n : 2 * n], *refs[2 * n :])
+    stages = ((0, ag.step0), (1, ag.step1), (2, ag.step2), (3, ag.step3), (4, ag.step4))
+    for t in range(n + 4):
+        for off, f in stages:
+            if 0 <= t - off < n:
+                f(t - off)
+    ag.finish()
+
+
+def gather(shards):
+    n = len(shards)
+    hbm = pl.BlockSpec(memory_space=pl.ANY)
+    return pl.pallas_call(
+        functools.partial(gather_kernel, n),
+        out_shape=[jax.ShapeDtypeStruct((4, 4, 2) + s.shape, s.dtype) for s in shards],
+        in_specs=[hbm] * n,
+        out_specs=[hbm] * n,
+        scratch_shapes=[
+            pltpu.SemaphoreType.DMA((n, 11)), pltpu.SemaphoreType.DMA((n, 11)), pltpu.SemaphoreType.DMA((n,)),
+        ],
+        compiler_params=pltpu.CompilerParams(collective_id=0, has_side_effects=True),
+    )(*shards)
+
+
+class Scatter:
+    def __init__(self, here, items, bufs, ssem, rsem, lsem, free):
+        self.h, self.items, self.bufs = here, items, bufs
+        self.ssem, self.rsem, self.lsem, self.free = ssem, rsem, lsem, free
+        self.sends = {}
+
+    def rc(self, i, k, src, dst, dev):
+        return pltpu.make_async_remote_copy(
+            src_ref=src, dst_ref=dst, send_sem=self.ssem.at[i, k], recv_sem=self.rsem.at[i, k],
+            device_id=dev, device_id_type=MESH,
+        )
+
+    def go(self, i, *moves):
+        for m in moves:
+            m.start()
+            self.sends.setdefault(i, []).append(m)
+
+    def views(self, i):
+        it = self.items[i]
+        return it, self.bufs[it["cls"]], it["slot"], it["w"]
+
+    def m_sib(self, i):
+        it, b, s, w = self.views(i)
+        src = it["g"].at[:, :, 1 - self.h.c, :, pl.ds(it["c0"], w)]
+        return self.rc(i, 0, src, b["r1"].at[s, :, :, :, 0:w], self.h.sib)
+
+    def m_load(self, i):
+        it, b, s, w = self.views(i)
+        src = it["g"].at[:, :, self.h.c, :, pl.ds(it["c0"], w)]
+        return pltpu.make_async_copy(src, b["p"].at[s, :, :, :, 0:w], self.lsem.at[i])
+
+    def m_dx(self, i):
+        it, b, s, w = self.views(i)
+        return self.rc(i, 1, b["p"].at[s, self.h.dg, 0:2, :, 0:w], b["rd"].at[s, 0, :, :, 0:w], self.h.xdev)
+
+    def m_dy(self, i):
+        it, b, s, w = self.views(i)
+        return self.rc(i, 2, b["p"].at[s, self.h.dg, 2:4, :, 0:w], b["rd"].at[s, 1, :, :, 0:w], self.h.ydev)
+
+    def m_x(self, i):
+        it, b, s, w = self.views(i)
+        return self.rc(i, 3, b["p"].at[s, self.h.nx, :, :, 0:w], b["rxy"].at[s, 0, :, :, 0:w], self.h.xdev)
+
+    def m_y(self, i):
+        it, b, s, w = self.views(i)
+        return self.rc(i, 4, b["p"].at[s, self.h.ny, :, :, 0:w], b["rxy"].at[s, 1, :, :, 0:w], self.h.ydev)
+
+    def m_z(self, i, k):
+        it, b, s, w = self.views(i)
+        return self.rc(
+            i, 5 + k, b["p"].at[s, self.h.dp, self.h.zp[k], :, 0:w], b["rz"].at[s, k, :, 0:w], self.h.zdev[k]
+        )
+
+    def step0(self, i):
+        it = self.items[i]
+        if it["wait_free"] is not None:
+            for m in self.sends.pop(it["wait_free"]):
+                m.wait_send()
+            for k in range(6):
+                pl.semaphore_wait(self.free.at[k], 1)
+        self.m_load(i).start()
+        self.go(i, self.m_sib(i))
+
+    def step1(self, i):
+        it, b, s, w = self.views(i)
+        p, r, dg = b["p"], b["r1"], self.h.dg
+        self.m_load(i).wait()
+        self.m_sib(i).wait_recv()
+
+        def far(j, _):
+            p[s, dg, j, :, 0:w] = p[s, dg, j, :, 0:w] + r[s, dg, j, :, 0:w]
+            return 0
+
+        lax.fori_loop(0, 4, far, 0)
+        self.go(i, self.m_dx(i), self.m_dy(i))
+
+        def near(j, _):
+            a, q = lax.rem(dg + 1 + lax.div(j, 4), 4), lax.rem(j, 4)
+            p[s, a, q, :, 0:w] = p[s, a, q, :, 0:w] + r[s, a, q, :, 0:w]
+            return 0
+
+        lax.fori_loop(0, 12, near, 0)
+
+    def step2(self, i):
+        it, b, s, w = self.views(i)
+        p, rd, nx, ny = b["p"], b["rd"], self.h.nx, self.h.ny
+        self.m_dx(i).wait_recv()
+
+        def to_y(j, _):
+            p[s, ny, j, :, 0:w] = p[s, ny, j, :, 0:w] + rd[s, 0, j, :, 0:w]
+            return 0
+
+        lax.fori_loop(0, 2, to_y, 0)
+        self.go(i, self.m_y(i))
+        self.m_dy(i).wait_recv()
+
+        def to_x(j, _):
+            p[s, nx, 2 + j, :, 0:w] = p[s, nx, 2 + j, :, 0:w] + rd[s, 1, j, :, 0:w]
+            return 0
+
+        lax.fori_loop(0, 2, to_x, 0)
+        self.go(i, self.m_x(i))
+
+    def step3(self, i):
+        it, b, s, w = self.views(i)
+        p, rxy, dp = b["p"], b["rxy"], self.h.dp
+        self.m_x(i).wait_recv()
+        self.m_y(i).wait_recv()
+
+        def own(j, _):
+            both = rxy[s, 0, j, :, 0:w].astype(f32) + rxy[s, 1, j, :, 0:w].astype(f32)
+            p[s, dp, j, :, 0:w] = (p[s, dp, j, :, 0:w].astype(f32) + both).astype(p.dtype)
+            return 0
+
+        lax.fori_loop(0, 4, own, 0)
+        self.go(i, *[self.m_z(i, k) for k in range(3)])
+
+    def step4(self, i):
+        it, b, s, w = self.views(i)
+        p, rz = b["p"], b["rz"]
+        for k in range(3):
+            self.m_z(i, k).wait_recv()
+        total = p[s, self.h.dp, self.h.z, :, 0:w].astype(f32)
+        for k in range(3):
+            total = total + rz[s, k, :, 0:w].astype(f32)
+        it["out"][:, it["oc"] : it["oc"] + w] = total
+        if it["signal_free"]:
+            for k, d in enumerate(self.h.peers):
+                pl.semaphore_signal(self.free.at[k if k < 3 else 8 - k], inc=1, device_id=d, device_id_type=MESH)
+
+    def finish(self):
+        for i in list(self.sends):
+            for m in self.sends.pop(i):
+                m.wait_send()
+
+
+def scatter_plan(specs, ring):
+    items, by_class = [], {}
+    for gi, c0, w, cls in specs:
+        mine = by_class.setdefault(cls, [])
+        it = dict(gi=gi, c0=c0, w=w, cls=cls, oc=c0, slot=len(mine) % ring[cls], wait_free=None, signal_free=False)
+        if len(mine) >= ring[cls]:
+            it["wait_free"] = mine[-ring[cls]]
+            items[it["wait_free"]]["signal_free"] = True
+        mine.append(len(items))
+        items.append(it)
+    return items
+
+
+SCATTER_BUFFERS = ("p", "r1", "rd", "rxy", "rz")
+
+
+def scatter_scratch(slots, r, w, dt):
+    return [
+        pltpu.VMEM((slots, 4, 4, r, w), dt), pltpu.VMEM((slots, 4, 4, r, w), dt), pltpu.VMEM((slots, 2, 2, r, w), dt),
+        pltpu.VMEM((slots, 2, 4, r, w), dt), pltpu.VMEM((slots, 3, r, w), dt),
+    ]
+
+
+def scatter_kernel(items, ng, classes, *refs):
+    gs, outs, rest = refs[:ng], refs[ng : 2 * ng], list(refs[2 * ng :])
+    bufs = {}
+    for cls in classes:
+        bufs[cls] = dict(zip(SCATTER_BUFFERS, rest[:5]))
+        rest = rest[5:]
+    here = Place()
+    here.barrier()
+    items = [dict(it, g=gs[it["gi"]], out=outs[it["gi"]]) for it in items]
+    rs = Scatter(here, items, bufs, *rest)
+    n = len(items)
+    for t in range(n + 4):
+        for off, f in enumerate((rs.step0, rs.step1, rs.step2, rs.step3, rs.step4)):
+            if 0 <= t - off < n:
+                f(t - off)
+    rs.finish()
+
+
+def reduce_scatter(gs, specs, ring, shapes):
+    items = scatter_plan(specs, ring)
+    n, classes, scratch = len(items), list(ring), []
+    for cls in classes:
+        scratch += scatter_scratch(ring[cls], *shapes[cls])
+    scratch += [
+        pltpu.SemaphoreType.DMA((n, 8)), pltpu.SemaphoreType.DMA((n, 8)), pltpu.SemaphoreType.DMA((n,)),
+        pltpu.SemaphoreType.REGULAR((6,)),
+    ]
+    return pl.pallas_call(
+        functools.partial(scatter_kernel, items, len(gs), classes),
+        out_shape=[jax.ShapeDtypeStruct(g.shape[3:], f32) for g in gs],
+        in_specs=[pl.BlockSpec(memory_space=pl.ANY)] * len(gs),
+        out_specs=[pl.BlockSpec(memory_space=pltpu.VMEM)] * len(gs),
+        scratch_shapes=scratch,
+        compiler_params=pltpu.CompilerParams(collective_id=1, has_side_effects=True, vmem_limit_bytes=58 * 2**20),
+    )(*gs)
+
+
+def blocks(grad):
+    return grad.reshape((4, 4, 2, grad.shape[0] // 32, grad.shape[1]))
+
+
+def column_parts(width, part):
+    return [(c0, min(part, width - c0)) for c0 in range(0, width, part)]
+
+
+def slice_body(
+    tokens, lengths, cotangent, w_query, w_key, w_value, w_gate, w_out, out_gain, w_first, w_second, w_down,
+):
+    slot_count, slot_len, feature_width = tokens.shape
+    row_count = slot_count * slot_len
+    ff_width = w_first.shape[1]
+    places = lax.broadcasted_iota(jnp.int32, (slot_count, slot_len), 1)
+    live_rows = (places < lengths[:, None]).astype(f32).reshape(row_count, 1)
+    me = lax.axis_index("dp") * 8 + lax.axis_index("fsdp")
+    lane = lax.broadcasted_iota(jnp.int32, (16, 128), 1)
+    gain_block = jnp.where(lax.div(lane, 32) == lax.rem(me, 4), jnp.tile(out_gain, 4)[None, :], 0)
+    full = gather((w_query, w_key, w_value, w_gate, gain_block, w_out, w_first, w_second, w_down))
+    gain_full = full[4].reshape(8, 4, 16, 128)[:, :, 0].sum(axis=1).reshape(feature_width)
+    query_full, key_full, value_full, gate_full, _, out_full, first_full, second_full, down_full = [
+        w.reshape(-1, w.shape[-1]) for w in full
+    ]
+    inputs = tokens.reshape(row_count, feature_width).astype(f32)
+    normed_in, inv_in = normalize(inputs)
+    first_in = normed_in.astype(bf16)
+    query_rows = project(first_in, query_full).astype(bf16)
+    key_rows = project(first_in, key_full).astype(bf16)
+    value_rows = project(first_in, value_full).astype(bf16)
+    gate_pre = project(first_in, gate_full)
+    head_mix, logsum = attend(query_rows, key_rows, value_rows)
+    normed_mix, inv_mix = normalize(head_mix)
+    gain_rows = gain_full.astype(f32)
+    gate_act = jax.nn.silu(gate_pre)
+    scaled_mix = normed_mix * gain_rows
+    branch_in = (scaled_mix * gate_act).astype(bf16)
+    middle = inputs + live_rows * project(branch_in, out_full)
+    normed_mid, inv_mid = normalize(middle)
+    second_in = normed_mid.astype(bf16)
+    first_proj = project(second_in, first_full)
+    second_proj = project(second_in, second_full)
+    hidden = (first_proj * second_proj).astype(bf16)
+    final_rows = middle + live_rows * project(hidden, down_full)
+    layer_out = final_rows.astype(bf16).reshape(tokens.shape)
+    grad_final = cotangent.reshape(row_count, feature_width).astype(f32)
+    grad_branch = (live_rows * grad_final).astype(bf16)
+    grad_hidden = project_back(grad_branch, down_full)
+    grad_first_proj = (grad_hidden * second_proj).astype(bf16)
+    grad_second_proj = (grad_hidden * first_proj).astype(bf16)
+    grad_normed_mid = project_back(grad_first_proj, first_full) + project_back(grad_second_proj, second_full)
+    grad_middle = grad_final + norm_back(normed_mid, inv_mid, grad_normed_mid)
+    grad_attn_out = (live_rows * grad_middle).astype(bf16)
+    grad_branch_in = project_back(grad_attn_out, out_full)
+    gain_terms = grad_branch_in * gate_act * normed_mix
+    sigmoid_gate = jax.nn.sigmoid(gate_pre)
+    grad_gate_pre = (
+        grad_branch_in * scaled_mix * sigmoid_gate * (1.0 + gate_pre * (1.0 - sigmoid_gate))
+    ).astype(bf16)
+    grad_scaled = grad_branch_in * gate_act * gain_rows
+    grad_mix = norm_back(normed_mix, inv_mix, grad_scaled).astype(bf16)
+    grad_queries, grad_keys, grad_values = attend_back(query_rows, key_rows, value_rows, logsum, grad_mix)
+    grad_normed_in = (
+        project_back(grad_queries, query_full) + project_back(grad_keys, key_full)
+        + project_back(grad_values, value_full) + project_back(grad_gate_pre, gate_full)
+    )
+    grad_inputs = grad_middle + norm_back(normed_in, inv_in, grad_normed_in)
+    input_grad = grad_inputs.astype(bf16).reshape(tokens.shape)
+    gain_part = gain_terms.reshape(row_count // 8, 8, feature_width).sum(axis=0)
+    gain_blocks = jnp.repeat(gain_part.reshape(8, 8, 128).transpose(1, 0, 2), 4, axis=0).reshape(4, 4, 2, 8, 128)
+    gs = [blocks(weight_grad(a, b).astype(bf16)) for a, b in (
+        (hidden, grad_branch), (second_in, grad_first_proj), (second_in, grad_second_proj),
+        (branch_in, grad_attn_out), (first_in, grad_gate_pre), (first_in, grad_queries),
+        (first_in, grad_keys), (first_in, grad_values),
+    )] + [gain_blocks]
+    specs = [(0, c0, w, "down") for c0, w in column_parts(feature_width, 512)]
+    for g in (1, 2):
+        specs += [(g, c0, w, "in") for c0, w in column_parts(ff_width, 1024)]
+    specs += [(g, 0, feature_width, "in") for g in (3, 4, 5, 6, 7)] + [(8, 0, 128, "gain")]
+    down, first, second, out, gate, query, key, value, gain = reduce_scatter(
+        gs, specs, {"down": 2, "in": 5, "gain": 1},
+        {"down": (w_down.shape[0], 512, bf16), "in": (w_query.shape[0], 1024, bf16), "gain": (8, 128, f32)},
+    )
+    gain = lax.dynamic_slice(gain.sum(axis=0), (lax.rem(me, 4) * 32,), (32,))
+    return layer_out, input_grad, query, key, value, gate, out, gain, first, second, down
+
+
 def solution(mesh):
+    fits = mesh.shape["dp"] == 4 and mesh.shape["fsdp"] == 8
     return jax.shard_map(
-        body,
+        slice_body if fits else general_body,
         mesh=mesh,
         in_specs=(
             P(("dp", "fsdp"), None, None),

time: 1350 us -> 657 us (0.49)
  waiting for transfers between devices: 897 us -> 0 us
  Pallas kernels: 0 us -> 281 us
  blocking collectives: 42.2 us -> 0 us
  matrix products: 214 us -> 200 us
    reduce_scatter x3 -> x0, waiting for transfers between devices: 572 us -> none  [the longest x1 248 us: ffn_sums(): lax.psum_scatter(weight_grad(second_in, both_proj), ('dp', 'fsdp'), scatt...]
    all_gather x8 -> x0, waiting for transfers between devices: 320 us -> none  [the longest x1 61.3 us: body(): lax.all_gather(w_second, ('dp', 'fsdp'), axis=0, tiled=True)]
    pallas_call x0 -> x2, Pallas kernels: none -> 281 us  [the longest x1 146 us: reduce_scatter(): pl.pallas_call(functools.partial(scatter_kernel, items, len(gs), classes)...]
    unnamed x1 -> x0, blocking collectives: 42.2 us -> none
    concatenate x1 -> x0, other arithmetic: 15.7 us -> none  [body(): jnp.concatenate([from_input, from_branch, gain_part], axis=1)]
    unnamed x60 -> x94, local copies, waits for them, and re-layouts: 21.9 us -> 30.3 us
    dot_general x4 -> x8, matrix products: 54.6 us -> 46.5 us  [weight_grad(): lax.dot_general(inputs, upstream, (((0,), (0,)), ((), ())), preferred_ele...]
    reshape x6 -> x7, local copies, waits for them, and re-layouts: 38.1 us -> 44.7 us  [split_heads(): return row_block.reshape(row_count // BLOCK, BLOCK, HEADS, HEAD_DIM)]
  transfers between devices with their start and end apart: 11 -> 0, of which waited for: 11 -> 0; matrix products, arithmetic and copies ran while one was open for 15% -> 0% of each run, Pallas kernels for 0% -> 0%
where the time goes in v1:
time: 657 us; the launch traced here: 646 us
  Pallas kernels  281 us (43%)
  matrix products  200 us (30%)
  local copies, waits for them, and re-layouts  137 us (21%)
  other arithmetic  26.7 us (4%)
    pallas_call x1, Pallas kernels, reduce_scatter(): pl.pallas_call(functools.partial(scatter_kernel, items, len(gs), classes)...  146 us
    pallas_call x1, Pallas kernels, gather(): pl.pallas_call(functools.partial(gather_kernel, n), out_shape=[jax.ShapeD...  136 us
    dot_general x8, matrix products, project_back(): lax.dot_general(upstream, weight, (((1,), (1,)), ((), ())), preferred_ele...  60.2 us
    dot_general x8, matrix products, project(): return jnp.dot(left_rows, right_rows, preferred_element_type=jnp.float32)  53.4 us
    dot_general x8, matrix products, weight_grad(): lax.dot_general(inputs, upstream, (((0,), (0,)), ((), ())), preferred_ele...  46.5 us
    reshape x7, local copies, waits for them, and re-layouts, split_heads(): return row_block.reshape(row_count // BLOCK, BLOCK, HEADS, HEAD_DIM)  44.7 us
    unnamed x94, local copies, waits for them, and re-layouts  30.3 us
    convert_element_type x2, local copies, waits for them, and re-layouts, attend_back(): grad_keys.reshape(row_count, -1).astype(jnp.bfloat16)  14.4 us

profile of v1, /device:TPU:0, one launch (start us, length us, event | category | flops | bytes accessed | tf_op | source)
XLA Modules:
  0.0 646.5 jit_solution(13420653642566493704)
XLA Ops:
  2.7 2.9 copy.42
  6.1 4.2 copy.49
  10.2 135.7 %shard_map.203 = (bf16[4,4,2,32,1024]{4,3,2,1,0:T(8,128)(2,1)}, bf16[4,4,2,32,1024]{4,3,2,1,0:T(8,128)(2,1)}, bf16[4,4,2,32,1024]{4,3,2,1,0:T(8,128)(2,1)}, bf16...) custom-call(bf16[32,1024]{1,0:T(8,128)(2,1)} %refs_0_.1, ...), custom_call_target="tpu_custom_call" | custom-call | tf_op jit(solution)/shard_map/pallas_call | solution.py:358
  146.8 5.3 convolution_convert_fusion.8
  152.1 6.4 reshape.264
  158.5 7.1 %copy.56 = bf16[16,64,16,64]{1,3,2,0:T(8,128)(2,1)} copy(bf16[16,64,16,64]{3,2,1,0:T(8,128)(2,1)} %reshape.264) | data formatting | bytes 4194304 | tf_op jit(solution)/shard_map/reshape | solution.py:46
  165.6 5.3 convolution_convert_fusion.9
  170.9 6.4 reshape.262
  177.3 5.3 convolution_convert_fusion.7
  182.6 6.6 %reshape.266 = bf16[16,64,16,64]{3,2,1,0:T(8,128)(2,1)} reshape(bf16[1024,1024]{1,0:T(8,128)(2,1)} %convolution_convert_fusion.7) | data formatting | bytes 4194304 | tf_op jit(solution)/shard_map/reshape | solution.py:46
  189.2 7.1 %copy.52 = bf16[16,64,16,64]{1,3,2,0:T(8,128)(2,1)} copy(bf16[16,64,16,64]{3,2,1,0:T(8,128)(2,1)} %reshape.266) | data formatting | bytes 4194304 | tf_op jit(solution)/shard_map/reshape | solution.py:46
  196.2 5.7 fusion.29
  202.0 2.9 fusion
  207.3 5.4 multiply_reduce_fusion.1
  212.7 9.8 %copy.47 = f32[16,64,16,64]{3,2,1,0:T(8,128)} copy(f32[16,64,16,64]{1,3,2,0:T(8,128)} %get-tuple-element.77) | data formatting | bytes 8388608 | tf_op jit(solution)/shard_map/bhij,bjhd->bihd/transpose | solution.py:65
  222.5 7.6 %reshape.267 = f32[1024,1024]{1,0:T(8,128)} reshape(f32[16,64,16,64]{3,2,1,0:T(8,128)} %copy.47) | data formatting | bytes 8388608 | tf_op jit(solution)/shard_map/reshape | solution.py:68
  230.1 7.3 %multiply_convert_fusion.9 = (bf16[1024,1024]{1,0:T(8,128)(2,1)S(1)}, f32[1024,1024]{1,0:T(8,128)}) fusion(f32[1024,1024]{1,0:T(8,128)} %reshape.267, f32[1024]{0:T(1024)S(1)} %bitcast_convert_fusion, f32[1024]{0:T(1024)S(1)} %rsqrt.29, bf16[1024,1024]{1,0:T(8,128)(2,1)} %bitcast.155, bf16[1,1024,1024]{1,2,0:T(8,128)(2,1)S(1)} %copy.42, ...), kind=kOutput, calls=%fused_computation.52 | convolution fusion | flops 2159017984 | bytes 14692352 | tf_op jit(solution)/shard_map/dot_general | solution.py:29
  237.5 2.7 multiply_reduce_fusion.4
  240.3 2.0 copy-done.8
  242.9 9.0 %fusion.66 = f32[1024,2816]{1,0:T(8,128)} fusion(bf16[1024,1024]{0,1:T(8,128)(2,1)S(1)} %multiply_convert_fusion.10, bf16[1024,2816]{1,0:T(8,128)(2,1)S(1)} %bitcast.168), kind=kOutput, calls=%fused_computation.102 | convolution fusion | flops 5905580032 | bytes 19398656 | tf_op jit(solution)/shard_map/dot_general | solution.py:29
  251.9 9.0 %fusion.65 = f32[1024,2816]{1,0:T(8,128)} fusion(bf16[1024,1024]{0,1:T(8,128)(2,1)S(1)} %multiply_convert_fusion.10, bf16[1024,2816]{1,0:T(8,128)(2,1)S(1)} %bitcast.172), kind=kOutput, calls=%fused_computation.101 | convolution fusion | flops 5905580032 | bytes 19398656 | tf_op jit(solution)/shard_map/dot_general | solution.py:29
  260.9 17.6 %multiply_convert_fusion = (bf16[1024,2816]{1,0:T(8,128)(2,1)}, bf16[1024,2816]{1,0:T(8,128)(2,1)}, bf16[1024,2816]{1,0:T(8,128)(2,1)}) fusion(f32[1024,2816]{1,0:T(8,128)} %fusion.65, f32[1024,2816]{1,0:T(8,128)} %fusion.66, bf16[2816,1024]{1,0:T(8,128)(2,1)} %bitcast.153, bf16[1,1024,1024]{1,2,0:T(8,128)(2,1)S(1)} %copy-done.7, f32[1024]{0:T(1024)S(1)} %fusion.60), kind=kOutput, calls=%fused_computation | convolution fusion | flops 5926027264 | bytes 48238592 | tf_op jit(solution)/shard_map/dot_general | solution.py:33
  278.5 11.5 %fusion.67 = f32[1024,1024]{0,1:T(8,128)} fusion(bf16[1024,2816]{1,0:T(8,128)(2,1)} %get-tuple-element.73, bf16[1024,2816]{1,0:T(8,128)(2,1)} %bitcast.169), kind=kOutput, calls=%fused_computation.103 | convolution fusion | flops 5905580032 | bytes 15728640 | tf_op jit(solution)/shard_map/dot_general | solution.py:33
  290.0 9.5 %fusion.49 = bf16[1,1024,1024]{1,2,0:T(8,128)(2,1)} fusion(f32[1024,1024]{0,1:T(8,128)S(1)} %copy-done.9, bf16[1024,2816]{1,0:T(8,128)(2,1)S(1)} %copy-done.15, bf16[2816,1024]{1,0:T(8,128)(2,1)} %bitcast.154, f32[1024]{0:T(1024)S(1)} %fusion.60), kind=kOutput, calls=%fused_computation.79 | convolution fusion | flops 5908725760 | bytes 17829888 | tf_op jit(solution)/shard_map/dot_general | solution.py:29
  299.4 12.2 %multiply_reduce_fusion.3 = (f32[1024]{0:T(1024)S(1)}, f32[1024,1024]{0,1:T(8,128)}) fusion(f32[1024,1024]{0,1:T(8,128)S(1)} %copy-done.9, f32[1024]{0:T(1024)S(1)} %add_rsqrt_fusion.1, f32[1024,1024]{0,1:T(8,128)} %fusion.67, bf16[1024,2816]{1,0:T(8,128)(2,1)} %get-tuple-element.71, bf16[1024,2816]{1,0:T(8,128)(2,1)} %bitcast.165), kind=kOutput, calls=%fused_computation.49 | convolution fusion | flops 5909773312 | bytes 24125440 | tf_op jit(solution)/shard_map/dot_general | solution.py:33
  311.6 8.0 %convolution_convert_fusion = bf16[1024,2816]{1,0:T(8,128)(2,1)} fusion(bf16[1024,1024]{0,1:T(8,128)(2,1)S(1)} %copy-done.24, bf16[1024,2816]{1,0:T(8,128)(2,1)S(1)} %copy-done.16), kind=kOutput, calls=%fused_computation.14 | convolution fusion | flops 5908463616 | bytes 13631488 | tf_op jit(solution)/shard_map/dot_general | solution.py:39
  319.6 8.1 %convolution_convert_fusion.1 = bf16[1024,2816]{1,0:T(8,128)(2,1)} fusion(bf16[1024,1024]{0,1:T(8,128)(2,1)S(1)} %copy-done.24, bf16[1024,2816]{1,0:T(8,128)(2,1)S(1)} %bitcast.149), kind=kOutput, calls=%fused_computation.15 | convolution fusion | flops 5908463616 | bytes 13631488 | tf_op jit(solution)/shard_map/dot_general | solution.py:39
  327.8 3.5 fusion.3
  331.3 8.5 %convolution_convert_fusion.2 = bf16[2816,1024]{1,0:T(8,128)(2,1)} fusion(bf16[1024,2816]{1,0:T(8,128)(2,1)S(1)} %copy-done.15, bf16[1,1024,1024]{1,2,0:T(8,128)(2,1)S(1)} %copy-done.7, f32[1024]{0:T(1024)S(1)} %fusion.60), kind=kOutput, calls=%fused_computation.16 | convolution fusion | flops 5911609344 | bytes 13635584 | tf_op jit(solution)/shard_map/dot_general | solution.py:39
  339.8 3.8 convolution_convert_fusion.6
  343.6 2.5 copy.63
  346.1 8.9 %multiply_reduce_fusion.2 = (f32[1024]{0:T(1024)S(1)}, f32[1024,1024]{1,0:T(8,128)S(1)}) fusion(f32[1024,1024]{1,0:T(8,128)} %reshape.267, f32[1024]{0:T(1024)S(1)} %bitcast_convert_fusion, f32[1024]{0:T(1024)S(1)} %rsqrt.29, f32[1024,1024]{1,0:T(8,128)} %get-tuple-element.79, bf16[1024,1024]{1,0:T(8,128)(2,1)} %bitcast.179, f32[1024,1024]{0,1:T(8,128)} %copy-done.10, ...), kind=kOutput, calls=%fused_computation.46 | convolution fusion | flops 2159016960 | bytes 18890752 | tf_op jit(solution)/shard_map/dot_general | solution.py:33
  355.0 1.7 bitcast_reduce_fusion
  356.7 4.3 multiply_convert_fusion.6
  361.7 3.9 reshape.275
  365.7 7.2 %copy.60 = bf16[16,64,16,64]{1,3,2,0:T(8,128)(2,1)} copy(bf16[16,64,16,64]{3,2,1,0:T(8,128)(2,1)} %reshape.275) | data formatting | bytes 4194304 | tf_op jit(solution)/shard_map/reshape | solution.py:46
  372.9 5.4 fusion.46
  378.3 7.7 %convert_bitcast_fusion.2 = bf16[16,64,16,64]{1,3,2,0:T(8,128)(2,1)} fusion(bf16[16,64,16,64]{1,3,2,0:T(8,128)(2,1)S(1)} %copy-done.6, f32[16,16,64]{2,1,0:T(8,128)S(1)} %copy-done.17, f32[16,16,64,64]{2,3,1,0:T(8,128)} %copy-done, pred[64,64]{0,1:T(8,128)(4,1)S(1)} %copy-done.26), kind=kOutput, calls=%fused_computation.44 | convolution fusion | flops 139460608 | bytes 8458240 | tf_op jit(solution)/shard_map/bhij,bihd->bjhd/dot_general | solution.py:81
  386.1 7.0 %copy.62 = bf16[16,64,16,64]{3,2,1,0:T(8,128)(2,1)} copy(bf16[16,64,16,64]{1,3,2,0:T(8,128)(2,1)} %convert_bitcast_fusion.2) | data formatting | bytes 4194304 | tf_op jit(solution)/shard_map/convert_element_type | solution.py:100
  393.1 6.5 %convert_element_type.206 = bf16[1024,1024]{1,0:T(8,128)(2,1)} reshape(bf16[16,64,16,64]{3,2,1,0:T(8,128)(2,1)} %copy.62) | data formatting | bytes 4194304 | tf_op jit(solution)/shard_map/convert_element_type | solution.py:100
  399.6 12.1 %multiply_reduce_fusion = (f32[16,16,64]{2,1,0:T(8,128)S(1)}, f32[16,16,64,64]{2,3,1,0:T(8,128)}) fusion(f32[16,16,64]{2,1,0:T(8,128)S(1)} %copy-done.17, f32[16,16,64,64]{2,3,1,0:T(8,128)} %copy-done, pred[64,64]{0,1:T(8,128)(4,1)S(1)} %copy-done.26, bf16[16,64,16,64]{1,3,2,0:T(8,128)(2,1)} %copy.60, bf16[16,64,16,64]{3,2,1,0:T(8,128)(2,1)} %reshape.262), kind=kOutput, calls=%fused_computation.6 | convolution fusion | flops 139444224 | bytes 12718080 | tf_op jit(solution)/shard_map/bihd,bjhd->bhij/dot_general | solution.py:78
  411.7 7.7 %multiply_convert_fusion.5 = bf16[16,16,64,64]{2,3,1,0:T(8,128)(2,1)S(1)} fusion(f32[16,16,64,64]{2,3,1,0:T(8,128)} %get-tuple-element.87, f32[16,16,64]{2,1,0:T(8,128)S(1)} %get-tuple-element.86, f32[16,16,64]{2,1,0:T(8,128)S(1)} %copy-done.17, f32[16,16,64,64]{2,3,1,0:T(8,128)} %copy-done, pred[64,64]{0,1:T(8,128)(4,1)S(1)} %copy-done.26), kind=kLoop, calls=%fused_computation.5 | loop fusion | flops 6291456 | bytes 10620928 | tf_op jit(solution)/shard_map/convert_element_type | solution.py:86
  419.4 4.3 fusion.22
  423.6 4.3 fusion.21
  428.0 7.7 %copy.55 = bf16[16,64,16,64]{3,2,1,0:T(8,128)(2,1)} copy(bf16[16,64,16,64]{3,1,2,0:T(8,128)(2,1)} %fusion.21) | data formatting | bytes 4194304 | tf_op jit(solution)/shard_map/convert_element_type | solution.py:98
  435.7 6.5 %convert_element_type.199 = bf16[1024,1024]{1,0:T(8,128)(2,1)} reshape(bf16[16,64,16,64]{3,2,1,0:T(8,128)(2,1)} %copy.55) | data formatting | bytes 4194304 | tf_op jit(solution)/shard_map/convert_element_type | solution.py:98
  442.2 7.7 %copy.59 = bf16[16,64,16,64]{3,2,1,0:T(8,128)(2,1)} copy(bf16[16,64,16,64]{3,1,2,0:T(8,128)(2,1)} %fusion.22) | data formatting | bytes 4194304 | tf_op jit(solution)/shard_map/convert_element_type | solution.py:99
  449.9 6.7 %convert_element_type.202 = bf16[1024,1024]{1,0:T(8,128)(2,1)} reshape(bf16[16,64,16,64]{3,2,1,0:T(8,128)(2,1)} %copy.59) | data formatting | bytes 4194304 | tf_op jit(solution)/shard_map/convert_element_type | solution.py:99
  456.6 5.4 convolution_convert_fusion.4
  462.0 2.4 fusion.69
  464.4 3.6 convolution_convert_fusion.5
  468.0 2.4 fusion.68
  470.4 3.7 convolution_convert_fusion.3
  474.1 2.4 fusion.70
  476.5 3.0 fusion.10
  479.6 2.7 fusion.40
  482.2 3.9 copy.64
  486.1 145.6 %shard_map.204 = (f32[88,1024]{1,0:T(8,128)}, f32[32,2816]{1,0:T(8,128)}, f32[32,2816]{1,0:T(8,128)}, f32[32,1024]{1,0:T(8,128)}, f32[32,1024]{1,0:T(8,128)}, /*...) custom-call(bf16[4,4,2,88,1024]{4,3,2,1,0:T(8,128)(2,1)} %bitcast.152, ...), custom_call_target="tpu_custom_call" | custom-call | tf_op jit(solution)/shard_map/pallas_call | solution.py:556
  633.0 1.6 copy.91
  634.6 1.6 copy.92
  639.3 1.6 copy.95
  640.8 1.7 copy.96
  642.6 1.7 copy.97
  644.3 1.7 copy.98
  (108 shorter events, 11.0 us)
Async XLA Ops:
  2.7 203.0 %copy-start.25 = (pred[64,64]{0,1:T(8,128)(4,1)}, pred[64,64]{0,1:T(8,128)(4,1)S(1)}, u32[]{:S(2)}) copy-start(pred[64,64]{0,1:T(8,128)(4,1)S(1)} %iota_compare_fusion) | copy-start | bytes 12292
  5.6 231.9 %copy-start.1 = (bf16[1,1024,1024]{1,2,0:T(8,128)(2,1)}, bf16[1,1024,1024]{1,2,0:T(8,128)(2,1)S(1)}, u32[]{:S(2)}) copy-start(bf16[1,1024,1024]{1,2,0:T(8,128)(2,1)S(1)} %copy.42) | copy-start | bytes 6291460
  6.1 224.1 %copy-start.27 = (f32[1024]{0:T(1024)}, f32[1024]{0:T(1024)S(1)}, u32[]{:S(2)}) copy-start(f32[1024]{0:T(1024)S(1)} %add_rsqrt_fusion.2) | copy-start | bytes 12292
  202.0 4.3 copy-start
  202.0 5.3 copy-start.12
  230.1 7.3 %copy-start.32 = (bf16[4,4,2,32,1024]{4,3,2,1,0:T(8,128)(2,1)S(1)}, bf16[4,4,2,32,1024]{4,3,2,1,0:T(8,128)(2,1)}, u32[]{:S(2)}) copy-start(bf16[4,4,2,32,1024]{4,3,2,1,0:T(8,128)(2,1)} %get-tuple-element.34) | copy-start | bytes 6291460
  237.4 2.8 copy-start.33
  237.4 5.4 slice-start.2
  237.5 5.4 slice-start.3
  240.2 2.0 copy-start.8
  242.2 9.6 %slice-start.4 = ((s8[5767168]{0:T(1024)(128)(4,1)}), s8[4194304]{0:T(1024)(128)(4,1)S(1)}, s32[]{:S(2)}) async-start(s8[5767168]{0:T(1024)(128)(4,1)} %bitcast.170), calls=%async_computation.4 | async-start | bytes 8388608
  242.8 9.0 %copy-start.23 = (bf16[1024,1024]{0,1:T(8,128)(2,1)}, bf16[1024,1024]{0,1:T(8,128)(2,1)S(1)}, u32[]{:S(2)}) copy-start(bf16[1024,1024]{0,1:T(8,128)(2,1)S(1)} %multiply_convert_fusion.10) | copy-start | bytes 6291460
  242.9 9.0 %slice-start.5 = ((s8[5767168]{0:T(1024)(128)(4,1)}), s8[1572864]{0:T(1024)(128)(4,1)S(1)}, s32[]{:S(2)}) async-start(s8[5767168]{0:T(1024)(128)(4,1)} %bitcast.170), calls=%async_computation.5 | async-start | bytes 3145728
  251.9 9.0 %copy-start.7 = (bf16[1,1024,1024]{1,2,0:T(8,128)(2,1)S(1)}, bf16[1,1024,1024]{1,2,0:T(8,128)(2,1)}, u32[]{:S(2)}) copy-start(bf16[1,1024,1024]{1,2,0:T(8,128)(2,1)} %copy.49) | copy-start | bytes 6291460
  278.4 11.5 %copy-start.9 = (f32[1024,1024]{0,1:T(8,128)S(1)}, f32[1024,1024]{0,1:T(8,128)}, u32[]{:S(2)}) copy-start(f32[1024,1024]{0,1:T(8,128)} %copy-done.8) | copy-start | bytes 12582916
  278.5 11.5 %copy-start.15 = (bf16[1024,2816]{1,0:T(8,128)(2,1)S(1)}, bf16[1024,2816]{1,0:T(8,128)(2,1)}, u32[]{:S(2)}) copy-start(bf16[1024,2816]{1,0:T(8,128)(2,1)} %get-tuple-element.72) | copy-start | bytes 17301508
  289.9 29.7 %slice-start = ((s8[5767168]{0:T(1024)(128)(4,1)}), s8[4194304]{0:T(1024)(128)(4,1)S(1)}, s32[]{:S(2)}) async-start(s8[5767168]{0:T(1024)(128)(4,1)} %bitcast.148), calls=%async_computation | async-start | bytes 8388608
  299.4 12.2 %copy-start.16 = (bf16[1024,2816]{1,0:T(8,128)(2,1)S(1)}, bf16[1024,2816]{1,0:T(8,128)(2,1)}, u32[]{:S(2)}) copy-start(bf16[1024,2816]{1,0:T(8,128)(2,1)} %get-tuple-element.71) | copy-start | bytes 17301508
  299.4 12.2 %copy-start.24 = (bf16[1024,1024]{0,1:T(8,128)(2,1)S(1)}, bf16[1024,1024]{0,1:T(8,128)(2,1)}, u32[]{:S(2)}) copy-start(bf16[1024,1024]{0,1:T(8,128)(2,1)} %copy-done.23) | copy-start | bytes 6291460
  299.4 20.2 %slice-start.1 = ((s8[5767168]{0:T(1024)(128)(4,1)}), s8[1572864]{0:T(1024)(128)(4,1)S(1)}, s32[]{:S(2)}) async-start(s8[5767168]{0:T(1024)(128)(4,1)} %bitcast.148), calls=%async_computation.1 | async-start | bytes 3145728
  331.2 8.5 %copy-start.10 = (f32[1024,1024]{0,1:T(8,128)}, f32[1024,1024]{0,1:T(8,128)S(1)}, u32[]{:S(2)}) copy-start(f32[1024,1024]{0,1:T(8,128)S(1)} %fusion.3) | copy-start | bytes 12582916
  331.2 8.5 %copy-start.34 = (bf16[1024,1024]{1,0:T(8,128)(2,1)S(1)}, bf16[1024,1024]{1,0:T(8,128)(2,1)}, u32[]{:S(2)}) copy-start(bf16[1024,1024]{1,0:T(8,128)(2,1)} %copy-done.33) | copy-start | bytes 6291460
  339.8 3.8 copy-start.22
  346.1 8.9 %copy-start.5 = (f32[1024,1024]{1,0:T(8,128)S(1)}, f32[1024,1024]{1,0:T(8,128)}, u32[]{:S(2)}) copy-start(f32[1024,1024]{1,0:T(8,128)} %reshape.267) | copy-start | bytes 12582916
  346.1 8.9 %copy-start.13 = (f32[1024,1024]{1,0:T(8,128)S(1)}, f32[1024,1024]{1,0:T(8,128)}, u32[]{:S(2)}) copy-start(f32[1024,1024]{1,0:T(8,128)} %get-tuple-element.79) | copy-start | bytes 12582916
  365.7 7.2 %copy-start.2 = (bf16[1,1024,1024]{1,2,0:T(8,128)(2,1)S(1)}, bf16[1,1024,1024]{1,2,0:T(8,128)(2,1)}, u32[]{:S(2)}) copy-start(bf16[1,1024,1024]{1,2,0:T(8,128)(2,1)} %copy-done.1) | copy-start | bytes 6291460
  365.7 7.2 %copy-start.28 = (f32[1024]{0:T(1024)S(1)}, f32[1024]{0:T(1024)}, u32[]{:S(2)}) copy-start(f32[1024]{0:T(1024)} %copy-done.27) | copy-start | bytes 12292
  372.9 5.4 copy-start.6
  372.9 5.4 copy-start.17
  372.9 5.4 copy-start.26
  411.7 7.7 %copy-start.3 = (bf16[16,64,16,64]{1,3,2,0:T(8,128)(2,1)S(1)}, bf16[16,64,16,64]{1,3,2,0:T(8,128)(2,1)}, u32[]{:S(2)}) copy-start(bf16[16,64,16,64]{1,3,2,0:T(8,128)(2,1)} %copy.56) | copy-start | bytes 6291460
  419.3 4.3 copy-start.4
  456.6 5.4 copy-start.21
  456.6 5.4 copy-start.31
  462.0 2.4 copy-start.20
  464.4 3.6 copy-start.30
  468.0 2.4 copy-start.19
  470.4 3.7 copy-start.29
  474.1 2.4 copy-start.14
  474.1 2.4 copy-start.18
  476.5 3.0 copy-start.11

commit v2 on v0

--- a/solution.py
+++ b/solution.py
@@ -1,8 +1,14 @@
+import functools
+from types import SimpleNamespace
+
 import jax
 import jax.numpy as jnp
 from jax import lax
+from jax.experimental import pallas as pl
+from jax.experimental.pallas import tpu as pltpu
 from jax.sharding import PartitionSpec as P
 
+AXES = ("dp", "fsdp")
 HEADS = 16
 HEAD_DIM = 64
 BLOCK = 64
@@ -100,16 +106,16 @@
 def ffn_sums(second_in, hidden, grad_first_proj, grad_second_proj, grad_branch):
     both_proj = jnp.concatenate([grad_first_proj, grad_second_proj], axis=1)
     inner_shard = lax.psum_scatter(
-        weight_grad(second_in, both_proj), ("dp", "fsdp"), scatter_dimension=0, tiled=True
+        weight_grad(second_in, both_proj), AXES, scatter_dimension=0, tiled=True
     )
     down_shard = lax.psum_scatter(
-        weight_grad(hidden, grad_branch), ("dp", "fsdp"), scatter_dimension=0, tiled=True
+        weight_grad(hidden, grad_branch), AXES, scatter_dimension=0, tiled=True
     )
     ff_width = grad_first_proj.shape[1]
     return (inner_shard[:, :ff_width], inner_shard[:, ff_width:], down_shard)
 
 
-def body(
+def general_body(
     tokens,
     lengths,
     cotangent,
@@ -128,17 +134,17 @@
     places = lax.broadcasted_iota(jnp.int32, (slot_count, slot_len), 1)
     live_rows = (places < lengths[:, None]).astype(jnp.float32).reshape(row_count, 1)
     attn_full = (
-        lax.all_gather(w_query, ("dp", "fsdp"), axis=0, tiled=True),
-        lax.all_gather(w_key, ("dp", "fsdp"), axis=0, tiled=True),
-        lax.all_gather(w_value, ("dp", "fsdp"), axis=0, tiled=True),
-        lax.all_gather(w_gate, ("dp", "fsdp"), axis=0, tiled=True),
-        lax.all_gather(w_out, ("dp", "fsdp"), axis=0, tiled=True),
-        lax.all_gather(out_gain, ("dp", "fsdp"), axis=0, tiled=True),
+        lax.all_gather(w_query, AXES, axis=0, tiled=True),
+        lax.all_gather(w_key, AXES, axis=0, tiled=True),
+        lax.all_gather(w_value, AXES, axis=0, tiled=True),
+        lax.all_gather(w_gate, AXES, axis=0, tiled=True),
+        lax.all_gather(w_out, AXES, axis=0, tiled=True),
+        lax.all_gather(out_gain, AXES, axis=0, tiled=True),
     )
     ffn_full = (
-        lax.all_gather(w_first, ("dp", "fsdp"), axis=0, tiled=True),
-        lax.all_gather(w_second, ("dp", "fsdp"), axis=0, tiled=True),
-        lax.all_gather(w_down, ("dp", "fsdp"), axis=0, tiled=True),
+        lax.all_gather(w_first, AXES, axis=0, tiled=True),
+        lax.all_gather(w_second, AXES, axis=0, tiled=True),
+        lax.all_gather(w_down, AXES, axis=0, tiled=True),
     )
     query_full, key_full, value_full, gate_full, out_full, gain_full = attn_full
     first_full, second_full, down_full = ffn_full
@@ -164,17 +170,17 @@
     final_rows = middle + live_rows * project(hidden, down_full)
     layer_out = final_rows.astype(jnp.bfloat16).reshape(tokens.shape)
     first_back, second_back, down_back = (
-        lax.all_gather(w_first, ("dp", "fsdp"), axis=0, tiled=True),
-        lax.all_gather(w_second, ("dp", "fsdp"), axis=0, tiled=True),
-        lax.all_gather(w_down, ("dp", "fsdp"), axis=0, tiled=True),
+        lax.all_gather(w_first, AXES, axis=0, tiled=True),
+        lax.all_gather(w_second, AXES, axis=0, tiled=True),
+        lax.all_gather(w_down, AXES, axis=0, tiled=True),
     )
     query_back, key_back, value_back, gate_back, out_back, gain_back = (
-        lax.all_gather(w_query, ("dp", "fsdp"), axis=0, tiled=True),
-        lax.all_gather(w_key, ("dp", "fsdp"), axis=0, tiled=True),
-        lax.all_gather(w_value, ("dp", "fsdp"), axis=0, tiled=True),
-        lax.all_gather(w_gate, ("dp", "fsdp"), axis=0, tiled=True),
-        lax.all_gather(w_out, ("dp", "fsdp"), axis=0, tiled=True),
-        lax.all_gather(out_gain, ("dp", "fsdp"), axis=0, tiled=True),
+        lax.all_gather(w_query, AXES, axis=0, tiled=True),
+        lax.all_gather(w_key, AXES, axis=0, tiled=True),
+        lax.all_gather(w_value, AXES, axis=0, tiled=True),
+        lax.all_gather(w_gate, AXES, axis=0, tiled=True),
+        lax.all_gather(w_out, AXES, axis=0, tiled=True),
+        lax.all_gather(out_gain, AXES, axis=0, tiled=True),
     )
     gain_used = gain_back.astype(jnp.float32)
     grad_final = cotangent.reshape(row_count, feature_width).astype(jnp.float32)
@@ -213,7 +219,7 @@
     gain_part = jnp.sum(gain_terms, axis=0)[:, None]
     attn_shard = lax.psum_scatter(
         jnp.concatenate([from_input, from_branch, gain_part], axis=1),
-        ("dp", "fsdp"),
+        AXES,
         scatter_dimension=0,
         tiled=True,
     )
@@ -239,36 +245,1168 @@
     )
 
 
+MESH = pl.DeviceIdType.MESH
+f32 = jnp.float32
+bf16 = jnp.bfloat16
+QUERY, KEY, VALUE, GATE, GAIN, OUT, FIRST, SECOND, DOWN = range(9)
+DOWN_PARTIAL = "down_partial"
+
+
+def bind(trees, refs):
+    fields = {}
+    for tree in trees:
+        leaves, form = jax.tree.flatten(tree)
+        fields |= jax.tree.unflatten(form, refs[: len(leaves)])
+        refs = refs[len(leaves) :]
+    return SimpleNamespace(**fields)
+
+
+class Place:
+    def __init__(self):
+        dp, fs = lax.axis_index(AXES[0]), lax.axis_index(AXES[1])
+        z, c = lax.div(fs, 2), lax.rem(fs, 2)
+        self.dp, self.fs, self.z, self.c = dp, fs, z, c
+        self.nx = dp + 1 - 2 * lax.rem(dp, 2)
+        self.ny = lax.rem(dp + 2, 4)
+        self.dg = lax.rem(self.nx + 2, 4)
+        self.zp = [lax.rem(z + k, 4) for k in (1, 2, 3)]
+        self.sib = (dp, z * 2 + 1 - c)
+        self.zdev = [(dp, zz * 2 + c) for zz in self.zp]
+        self.xdev, self.ydev = (self.nx, fs), (self.ny, fs)
+        self.peers = [self.sib, self.xdev, self.ydev] + self.zdev
+
+    def barrier(self):
+        bar = pltpu.get_barrier_semaphore()
+        for d in self.peers:
+            pl.semaphore_signal(bar, inc=1, device_id=d, device_id_type=MESH)
+        pl.semaphore_wait(bar, 6)
+
+
+class Gather:
+    def __init__(self, here, items, shards, outs, ssem, rsem, lsem):
+        self.h, self.items, self.shards, self.outs = here, items, shards, outs
+        self.ssem, self.rsem, self.lsem = ssem, rsem, lsem
+        self.sends = []
+
+    def rc(self, i, k, src, dst, dev):
+        return pltpu.make_async_remote_copy(
+            src_ref=src, dst_ref=dst, send_sem=self.ssem.at[i, k], recv_sem=self.rsem.at[i, k],
+            device_id=dev, device_id_type=MESH,
+        )
+
+    def go(self, m):
+        m.start()
+        self.sends.append(m)
+
+    def shard(self, i):
+        m, c0, w = self.items[i]
+        return self.shards[m].at[:, pl.ds(c0, w)]
+
+    def block(self, i, yx, z):
+        m, c0, w = self.items[i]
+        return self.outs[m].at[yx, z, self.h.c, :, pl.ds(c0, w)]
+
+    def own(self, i):
+        return pltpu.make_async_copy(self.shard(i), self.block(i, self.h.dp, self.h.z), self.lsem.at[i])
+
+    def zmsg(self, i, k):
+        return self.rc(i, k, self.shard(i), self.block(i, self.h.dp, self.h.z), self.h.zdev[k])
+
+    def col(self, i, k, yx, dev):
+        r = self.block(i, yx, slice(None))
+        return self.rc(i, k, r, r, dev)
+
+    def half(self, i, k, yx, lo, dev):
+        r = self.block(i, yx, slice(lo, lo + 2))
+        return self.rc(i, k, r, r, dev)
+
+    def step0(self, i):
+        self.own(i).start()
+        for k in range(3):
+            self.go(self.zmsg(i, k))
+
+    def step1(self, i):
+        h = self.h
+        self.own(i).wait()
+        for k in range(3):
+            self.zmsg(i, k).wait_recv()
+        self.go(self.col(i, 3, h.dp, h.xdev))
+        self.go(self.col(i, 4, h.dp, h.ydev))
+        self.go(self.col(i, 7, h.dp, h.sib))
+
+    def step2(self, i):
+        h = self.h
+        self.col(i, 3, h.dp, h.xdev).wait_recv()
+        self.go(self.half(i, 6, h.nx, 2, h.ydev))
+        self.go(self.col(i, 8, h.nx, h.sib))
+        self.col(i, 4, h.dp, h.ydev).wait_recv()
+        self.go(self.half(i, 5, h.ny, 0, h.xdev))
+        self.go(self.col(i, 9, h.ny, h.sib))
+
+    def step3(self, i):
+        h = self.h
+        self.half(i, 5, h.ny, 0, h.xdev).wait_recv()
+        self.half(i, 6, h.nx, 2, h.ydev).wait_recv()
+        self.go(self.col(i, 10, h.dg, h.sib))
+
+    def step4(self, i):
+        h = self.h
+        for k in (7, 8, 9, 10):
+            self.col(i, k, h.dp, h.sib).wait_recv()
+
+    def finish(self):
+        for m in self.sends:
+            m.wait_send()
+
+
+def column_parts(width, part):
+    return [(c0, min(part, width - c0)) for c0 in range(0, width, part)]
+
+
+def dot_nn(a, b):
+    return jnp.dot(a, b, preferred_element_type=f32)
+
+
+def dot_nt(a, b):
+    return lax.dot_general(a, b, (((1,), (1,)), ((), ())), preferred_element_type=f32)
+
+
+def dot_tn(a, b):
+    return lax.dot_general(a, b, (((0,), (0,)), ((), ())), preferred_element_type=f32)
+
+
+def tiles(count, body):
+    def step(i, carry):
+        body(i)
+        return carry
+
+    lax.fori_loop(0, count, step, 0)
+
+
+def rows_of(i, size):
+    return pl.ds(pl.multiple_of(i * size, size), size)
+
+
+def rms_inv(values):
+    return lax.rsqrt(jnp.mean(values * values, axis=-1, keepdims=True) + epsilon)
+
+
+QUAD = 4 * HEAD_DIM
+
+
+def quad_mask():
+    shape = (QUAD, QUAD)
+    row = lax.div(lax.broadcasted_iota(jnp.int32, shape, 0), HEAD_DIM)
+    return row == lax.div(lax.broadcasted_iota(jnp.int32, shape, 1), HEAD_DIM)
+
+
+def spread_heads(rows, mask):
+    tall = jnp.concatenate([rows] * 4, axis=0)
+    return jnp.where(mask, tall, jnp.zeros_like(tall))
+
+
+def per_head(values, reduce, fill):
+    halves = []
+    for k in range(2):
+        part = values[:, 128 * k : 128 * (k + 1)]
+        low = lax.broadcasted_iota(jnp.int32, part.shape, 1) < HEAD_DIM
+        first = reduce(jnp.where(low, part, fill), axis=-1, keepdims=True)
+        second = reduce(jnp.where(low, fill, part), axis=-1, keepdims=True)
+        halves.append(jnp.where(low, first, second))
+    return jnp.concatenate(halves, axis=1)
+
+
+def attend_blocks(b, q, k, v, probs, mix):
+    mask = quad_mask()
+    place = lax.broadcasted_iota(jnp.int32, (BLOCK, QUAD), 0)
+    causal = place >= lax.rem(lax.broadcasted_iota(jnp.int32, (BLOCK, QUAD), 1), HEAD_DIM)
+    at = [
+        (rows_of(2 * b + n, BLOCK), slice(QUAD * g, QUAD * (g + 1))) for n in range(2) for g in range(HEADS // 4)
+    ]
+    scores = [
+        jnp.where(causal, dot_nt(q[i], spread_heads(k[i], mask)) * HEAD_DIM ** (-0.5), masked_score) for i in at
+    ]
+    tops = [per_head(s, jnp.max, masked_score) for s in scores]
+    terms = [jnp.exp(s - m) for s, m in zip(scores, tops)]
+    totals = [per_head(t, jnp.sum, 0.0) for t in terms]
+    lows = [(t / n).astype(bf16) for t, n in zip(terms, totals)]
+    mixes = [dot_nn(p, spread_heads(v[i], mask)) for i, p in zip(at, lows)]
+    for i, p, m in zip(at, lows, mixes):
+        probs[i] = p
+        mix[i] = m
+
+
+def attend_blocks_back(b, q, k, v, probs, grad_mix, dq, dk, dv):
+    mask = quad_mask()
+    scale = HEAD_DIM ** (-0.5)
+    low = lax.broadcasted_iota(jnp.int32, (BLOCK, 128), 1) < HEAD_DIM
+
+    def own_head(wide):
+        return jnp.concatenate(
+            [
+                jnp.where(low, wide[0:64, 0:128], wide[64:128, 0:128]),
+                jnp.where(low, wide[128:192, 128:256], wide[192:256, 128:256]),
+            ],
+            axis=1,
+        )
+
+    at = [
+        (rows_of(2 * b + n, BLOCK), slice(QUAD * g, QUAD * (g + 1))) for n in range(2) for g in range(HEADS // 4)
+    ]
+    dps = [dot_nt(grad_mix[i], spread_heads(v[i], mask)) for i in at]
+    dvs = [own_head(dot_tn(probs[i], grad_mix[i])) for i in at]
+    ps = [probs[i].astype(f32) for i in at]
+    means = [per_head(dp * p, jnp.sum, 0.0) for dp, p in zip(dps, ps)]
+    dss = [(p * (dp - m)).astype(bf16) for p, dp, m in zip(ps, dps, means)]
+    dqs = [dot_nn(ds, spread_heads(k[i], mask)) * scale for i, ds in zip(at, dss)]
+    dks = [own_head(dot_tn(ds, q[i])) * scale for i, ds in zip(at, dss)]
+    for i, a, c, d in zip(at, dqs, dks, dvs):
+        dq[i] = a.astype(bf16)
+        dk[i] = c.astype(bf16)
+        dv[i] = d.astype(bf16)
+
+
+class Saves:
+    def __init__(self, sems):
+        self.sems, self.count, self.open = sems, 0, {}
+
+    def start(self, name, src, dst):
+        m = pltpu.make_async_copy(src, dst, self.sems.at[self.count])
+        self.count += 1
+        m.start()
+        self.open[name] = m
+
+    def wait(self, *names):
+        for name in names:
+            if name in self.open:
+                self.open.pop(name).wait()
+
+    def finish(self):
+        self.wait(*list(self.open))
+
+
+FORWARD_COPIES = 64
+X, DF, A1, Q, K, V, PB, GP, H, O, Y, A2, GAINS, SLABS = range(10, 24)
+
+
+def forward_kernel(items, trees, *refs):
+    ref = bind(trees, refs)
+    rows, width = ref.tokens.shape
+    ff = ref.shards[FIRST].shape[1]
+    parts = column_parts(ff, width)
+    x, a1, q, k, v, pb, h, a2, e0, e1, e2, df = [ref.page.at[i] for i in range(12)]
+    weight = [ref.weight.at[i] for i in range(4)]
+    hidden, first, second = (e0, e1, e2), (q, k, v), (pb, h, x)
+    wide = ref.wide
+    gate_rows, mix_rows, mid_rows = [pl.ds(rows * i, rows) for i in range(3)]
+    gp, o, y = wide.at[gate_rows], wide.at[mix_rows], wide.at[mid_rows]
+    here = Place()
+    here.barrier()
+    ag = Gather(here, items, ref.shards, ref.full, ref.ssem, ref.rsem, ref.lsem)
+    cp = Saves(ref.csem)
+    size = 128
+    live_len = ref.lengths[0]
+
+    def live(i, n):
+        return lax.broadcasted_iota(jnp.int32, (n, 1), 0) + i * n < live_len
+
+    def spread(values):
+        return jnp.broadcast_to(values, (values.shape[0], 128))
+
+    cp.start(X, ref.tokens, x)
+    cp.start(DF, ref.cotangent, df)
+
+    def norm_in():
+        cp.wait(X)
+
+        def tile(i):
+            r = rows_of(i, size)
+            t = x[r, :].astype(f32)
+            inv = rms_inv(t)
+            a1[r, :] = (t * inv).astype(bf16)
+            ref.inv_in[r, :] = spread(inv)
+
+        tiles(rows // size, tile)
+        cp.start(A1, a1, ref.save_a1)
+
+    def mask_df():
+        cp.wait(DF)
+
+        def tile(i):
+            r = rows_of(i, size)
+            df[r, :] = jnp.where(live(i, size), df[r, :], jnp.zeros((), bf16))
+
+        tiles(rows // size, tile)
+
+    def load(slot, m, c0=0, w=None):
+        src = ref.full[m]
+        w = src.shape[-1] if w is None else w
+        cp.start(slot, src.at[:, :, :, :, pl.ds(c0, w)], weight[slot].at[:, :, :, :, pl.ds(0, w)])
+
+    def matrix(slot, w=None):
+        w = width if w is None else w
+        return weight[slot][:, :, :, :, 0:w].reshape(width, w)
+
+    def projected(slot, dst, name=None, kept=None):
+        def run():
+            cp.wait(slot)
+
+            def tile(i):
+                r = rows_of(i, rows // 2)
+                dst[r, :] = dot_nn(a1[r, :], matrix(slot)).astype(dst.dtype)
+
+            tiles(2, tile)
+            if kept is not None:
+                cp.start(name, dst, kept)
+
+        return run
+
+    def gate_low():
+        def tile(i):
+            r = rows_of(i, size)
+            e0[r, :] = gp[r, :].astype(bf16)
+
+        tiles(rows // size, tile)
+        cp.start(GP, e0, ref.save_gp)
+
+    def attention(n, count):
+        def run():
+            tiles(count, lambda b: attend_blocks(b + n * count, q, k, v, pb, o))
+
+        return run
+
+    def mixed():
+        cp.start(PB, pb, ref.save_pb)
+        cp.wait(GAINS)
+        gains = ref.gain
+        gain = jnp.concatenate(
+            [
+                sum(gains[g, j, cc, 0:1, :].astype(f32) for j in (2 * half, 2 * half + 1) for cc in range(2))
+                for g in range(4)
+                for half in range(2)
+            ],
+            axis=1,
+        )
+
+        def tile(i):
+            r = rows_of(i, size)
+            t, z = o[r, :], gp[r, :]
+            inv = rms_inv(t)
+            h[r, :] = (t * inv * gain * (z * jax.nn.sigmoid(z))).astype(bf16)
+            e1[r, :] = t.astype(bf16)
+            ref.inv_mix[r, :] = spread(inv)
+
+        tiles(rows // size, tile)
+        cp.start(H, h, ref.save_h)
+        cp.start(O, e1, ref.save_o)
+
+    def middle(slot):
+        def run():
+            cp.wait(slot)
+
+            def tile(i):
+                r = rows_of(i, rows // 2)
+                y[r, :] = dot_nn(h[r, :], matrix(slot))
+
+            tiles(2, tile)
+
+            def norm(i):
+                r = rows_of(i, size)
+                t = x[r, :].astype(f32) + jnp.where(live(i, size), y[r, :], 0.0)
+                inv = rms_inv(t)
+                y[r, :] = t
+                a2[r, :] = (t * inv).astype(bf16)
+                ref.inv_mid[r, :] = spread(inv)
+
+            tiles(rows // size, norm)
+            cp.start(Y, y, ref.save_y)
+            cp.start(A2, a2, ref.save_a2)
+
+        return run
+
+    def gated(j, s1, s2, half):
+        c0, w = parts[j]
+        saved = ((first[j], ref.save_g1), (second[j], ref.save_g2), (hidden[j], ref.save_e))
+
+        def run():
+            if half == 0:
+                cp.wait(s1, s2, Q, K, V, PB, H, GP, O)
+            r = pl.ds(half * (rows // 2), rows // 2)
+            up = dot_nn(a2[r, :], matrix(s1, w))
+            first[j][r, 0:w] = up.astype(bf16)
+            other = dot_nn(a2[r, :], matrix(s2, w))
+            second[j][r, 0:w] = other.astype(bf16)
+            hidden[j][r, 0:w] = (up * other).astype(bf16)
+            if half == 1:
+                for n, (page, kept) in enumerate(saved):
+                    cp.start((j, n), page.at[:, 0:w], kept.at[:, pl.ds(c0, w)])
+
+        return run
+
+    def down_grad(j, c0, w):
+        def run():
+            if j == 2:
+                cp.wait(Y)
+            wide[pl.ds(parts[j][0] + c0, w), :] = dot_tn(hidden[j][:, c0 : c0 + w], df[...])
+
+        return run
+
+    def down_slabs():
+        slabs = ref.slabs
+        n = slabs.shape[1]
+
+        def tile(d):
+            slabs[d] = wide[pl.ds(pl.multiple_of(d * n, 8), n), :].astype(bf16)
+
+        tiles(slabs.shape[0], tile)
+        cp.start(SLABS, slabs, ref.down_partial)
+
+    work = [((), norm_in), ((), mask_df)]
+    work += [((0,), projected(0, q, Q, ref.save_q)), ((1,), projected(1, k, K, ref.save_k)), ((2,), projected(2, v, V, ref.save_v))]
+    work += [((), attention(n, 2)) for n in range(rows // BLOCK // 4)]
+    work += [((3,), projected(3, gp)), ((), gate_low), ((4,), mixed), ((5,), middle(0))]
+    slots = ((1, 2), (3, 0), (1, 2))
+    for j, (s1, s2) in enumerate(slots):
+        work += [((6 + 2 * j, 7 + 2 * j), gated(j, s1, s2, half)) for half in range(2)]
+    for j, (c0, w) in enumerate(parts):
+        step = 512 if w % 512 == 0 else w // 2
+        work += [((), down_grad(j, n * step, step)) for n in range(w // step)]
+    work += [((), down_slabs)]
+    loads = {0: (0, QUERY), 1: (1, KEY), 2: (2, VALUE), 3: (3, GATE), 5: (0, OUT)}
+    for j, (s1, s2) in enumerate(slots):
+        loads[6 + 2 * j] = (s1, FIRST) + parts[j]
+        loads[7 + 2 * j] = (s2, SECOND) + parts[j]
+    readers = {i: sum(i in needs for needs, _ in work) for i in range(len(items))}
+    ready, waiting, held = set(), [], {}
+
+    def try_loads():
+        while waiting:
+            i = waiting[0]
+            slot = loads[i][0]
+            if slot in held and readers[held[slot]]:
+                return
+            held[slot] = i
+            load(*loads[i])
+            ready.add(i)
+            waiting.pop(0)
+
+    def completed(i):
+        if i in loads:
+            waiting.append(i)
+            try_loads()
+        elif i == 4:
+            cp.start(GAINS, ref.full[GAIN], ref.gain)
+            ready.add(i)
+
+    def run_one():
+        if work and all(i in ready for i in work[0][0]):
+            needs, f = work.pop(0)
+            f()
+            for i in needs:
+                readers[i] -= 1
+            try_loads()
+
+    n = len(items)
+    stages = ((0, ag.step0), (1, ag.step1), (2, ag.step2), (3, ag.step3), (4, ag.step4))
+    for t in range(n + 4):
+        for off, f in stages:
+            if 0 <= t - off < n:
+                f(t - off)
+                if off == 4:
+                    completed(t - off)
+            if t > 0:
+                run_one()
+    while work:
+        run_one()
+    ag.finish()
+    cp.start(X, ref.inv_in, ref.save_inv_in)
+    cp.start(PB, ref.inv_mix, ref.save_inv_mix)
+    cp.start(Y, ref.inv_mid, ref.save_inv_mid)
+    cp.finish()
+
+
+def forward(tokens, lengths, cotangent, shards):
+    rows, width = tokens.shape
+    ff = shards[FIRST].shape[1]
+    parts = column_parts(ff, width)
+    items = [(m, 0, shards[m].shape[1]) for m in (QUERY, KEY, VALUE, GATE, GAIN, OUT)]
+    items += [(m, c0, w) for c0, w in parts for m in (FIRST, SECOND)]
+    items += [(DOWN, c0, w) for c0, w in column_parts(width, 256)]
+    n = len(items)
+    page, row = jax.ShapeDtypeStruct((rows, width), bf16), jax.ShapeDtypeStruct((rows, 128), f32)
+    wide = jax.ShapeDtypeStruct((rows, ff), bf16)
+    saves = dict(
+        save_a1=page, save_q=page, save_k=page, save_v=page, save_pb=page, save_gp=page, save_o=page, save_h=page,
+        save_a2=page, save_g1=wide, save_g2=wide, save_e=wide, save_y=jax.ShapeDtypeStruct((rows, width), f32),
+        save_inv_in=row, save_inv_mix=row, save_inv_mid=row,
+    )
+    slab = (32,) + shards[DOWN].shape
+    saves[DOWN_PARTIAL] = jax.ShapeDtypeStruct(slab, bf16)
+    outs = dict(full=[jax.ShapeDtypeStruct((4, 4, 2) + s.shape, bf16) for s in shards])
+    inv = pltpu.VMEM((rows, 128), f32)
+    scratch = dict(
+        page=pltpu.VMEM((12, rows, width), bf16),
+        weight=pltpu.VMEM((4, 4, 4, 2, shards[QUERY].shape[0], width), bf16),
+        wide=pltpu.VMEM((3 * rows, width), f32),
+        slabs=pltpu.VMEM(slab, bf16),
+        gain=pltpu.VMEM((4, 4, 2) + shards[GAIN].shape, bf16),
+        inv_in=inv, inv_mix=inv, inv_mid=inv,
+        ssem=pltpu.SemaphoreType.DMA((n, 11)),
+        rsem=pltpu.SemaphoreType.DMA((n, 11)),
+        lsem=pltpu.SemaphoreType.DMA((n,)),
+        csem=pltpu.SemaphoreType.DMA((FORWARD_COPIES,)),
+    )
+    ins = dict(cotangent=cotangent, shards=list(shards), tokens=tokens)
+    hbm = pl.BlockSpec(memory_space=pl.ANY)
+    leaves = jax.tree.leaves
+    got = pl.pallas_call(
+        functools.partial(forward_kernel, items, (dict(lengths=0), ins, outs, saves, scratch)),
+        out_shape=leaves(outs) + leaves(saves),
+        in_specs=[pl.BlockSpec(memory_space=pltpu.SMEM)] + [hbm] * len(leaves(ins)),
+        out_specs=[hbm] * len(leaves(outs) + leaves(saves)),
+        scratch_shapes=leaves(scratch),
+        compiler_params=pltpu.CompilerParams(
+            collective_id=0, has_side_effects=True, vmem_limit_bytes=62 * 2**20
+        ),
+    )(lengths, *leaves(ins))
+    full = got[: len(shards)]
+    return full, jax.tree.unflatten(jax.tree.structure(saves), got[len(shards) :])
+
+
+class Timeline:
+    def __init__(self, steps, work, window, given, after):
+        self.steps, self.work, self.window, self.after = steps, list(work), window, after
+        self.made = set(given)
+        self.at = [0] * len(steps)
+        self.when = [0.0] * len(steps)
+        self.free = {}
+        self.now = 0.0
+        self.done = set()
+        self.log = []
+
+    def next_steps(self):
+        started = 0
+        for i, at in enumerate(self.at):
+            if at == 0:
+                if i in self.made and started < self.window and self.after[i] <= self.done:
+                    yield i
+                return
+            if at < len(self.steps[i]):
+                started += at < 2
+                yield i
+
+    def step(self, i):
+        run, link, link_us, core_us = self.steps[i][self.at[i]]
+        self.now = max(self.now, self.when[i])
+        run(i)
+        self.now += core_us
+        begin = max(self.now, self.free.get(link, 0.0))
+        if link:
+            self.free[link] = begin + link_us
+        self.when[i] = begin + link_us + (1.5 if link else 0.0)
+        self.at[i] += 1
+        if self.at[i] == len(self.steps[i]):
+            self.done.add(i)
+        self.log.append((round(self.now, 1), "step", i, self.at[i] - 1))
+
+    def run(self):
+        while True:
+            steps = list(self.next_steps())
+            ready = [i for i in steps if self.when[i] <= self.now]
+            if ready:
+                self.step(ready[0])
+            elif self.work and all(n in self.done for n in self.work[0][2]):
+                run, core_us, _, gives = self.work.pop(0)
+                run()
+                self.now += core_us
+                if gives is not None:
+                    self.made.add(gives)
+                    self.when[gives] = self.now
+                self.log.append((round(self.now, 1), "work", getattr(run, "__name__", "")))
+            elif steps:
+                self.step(min(steps, key=lambda i: self.when[i]))
+            else:
+                return
+
+
+class Scatter:
+    def __init__(self, here, items, bufs, ssem, rsem, lsem, free):
+        self.h, self.items, self.bufs = here, items, bufs
+        self.ssem, self.rsem, self.lsem, self.free = ssem, rsem, lsem, free
+        self.sends = {}
+
+    def rc(self, i, k, src, dst, dev):
+        return pltpu.make_async_remote_copy(
+            src_ref=src, dst_ref=dst, send_sem=self.ssem.at[i, k], recv_sem=self.rsem.at[i, k],
+            device_id=dev, device_id_type=MESH,
+        )
+
+    def go(self, i, *moves):
+        for m in moves:
+            m.start()
+            self.sends.setdefault(i, []).append(m)
+
+    def views(self, i):
+        it = self.items[i]
+        return it, self.bufs[it.cls], it.slot, it.w
+
+    def mine(self, i, yx, z):
+        it, b, s, w = self.views(i)
+        if b.p is not None:
+            return b.p.at[s, yx, z, :, 0:w]
+        return b.g.at[s, yx, z, self.h.c, :, 0:w]
+
+    def m_sib(self, i):
+        it, b, s, w = self.views(i)
+        if b.p is not None:
+            src = it.src.at[:, :, 1 - self.h.c, :, pl.ds(it.c0, w)]
+        else:
+            src = b.g.at[s, :, :, 1 - self.h.c, :, 0:w]
+        return self.rc(i, 0, src, b.r1.at[s, :, :, :, 0:w], self.h.sib)
+
+    def m_load(self, i):
+        it, b, s, w = self.views(i)
+        src = it.src.at[:, :, self.h.c, :, pl.ds(it.c0, w)]
+        return pltpu.make_async_copy(src, b.p.at[s, :, :, :, 0:w], self.lsem.at[i])
+
+    def m_dx(self, i):
+        it, b, s, w = self.views(i)
+        return self.rc(i, 1, self.mine(i, self.h.dg, slice(0, 2)), b.rd.at[s, 0, :, :, 0:w], self.h.xdev)
+
+    def m_dy(self, i):
+        it, b, s, w = self.views(i)
+        return self.rc(i, 2, self.mine(i, self.h.dg, slice(2, 4)), b.rd.at[s, 1, :, :, 0:w], self.h.ydev)
+
+    def m_x(self, i):
+        it, b, s, w = self.views(i)
+        return self.rc(i, 3, self.mine(i, self.h.nx, slice(None)), b.rxy.at[s, 0, :, :, 0:w], self.h.xdev)
+
+    def m_y(self, i):
+        it, b, s, w = self.views(i)
+        return self.rc(i, 4, self.mine(i, self.h.ny, slice(None)), b.rxy.at[s, 1, :, :, 0:w], self.h.ydev)
+
+    def m_z(self, i, k):
+        it, b, s, w = self.views(i)
+        return self.rc(i, 5 + k, self.mine(i, self.h.dp, self.h.zp[k]), b.rz.at[s, k, :, 0:w], self.h.zdev[k])
+
+    def add(self, i, yx, z, *terms):
+        p = self.mine(i, yx, z)
+        total = p[...].astype(f32)
+        for t in terms:
+            total = total + t[...].astype(f32)
+        p[...] = total.astype(p.dtype)
+
+    def release(self, i):
+        for m in self.sends.pop(i):
+            m.wait_send()
+
+    def step0(self, i):
+        it, b, s, w = self.views(i)
+        if it.before is not None:
+            if b.p is not None:
+                self.release(it.before)
+            for k in range(6):
+                pl.semaphore_wait(self.free.at[it.cls, k], 1)
+        if b.p is not None:
+            self.m_load(i).start()
+        self.go(i, self.m_sib(i))
+
+    def step1(self, i):
+        it, b, s, w = self.views(i)
+        r, dg = b.r1, self.h.dg
+        if b.p is not None:
+            self.m_load(i).wait()
+        self.m_sib(i).wait_recv()
+        tiles(4, lambda j: self.add(i, dg, j, r.at[s, dg, j, :, 0:w]))
+        self.go(i, self.m_dx(i), self.m_dy(i))
+
+        def near(j):
+            a, q = lax.rem(dg + 1 + lax.div(j, 4), 4), lax.rem(j, 4)
+            self.add(i, a, q, r.at[s, a, q, :, 0:w])
+
+        tiles(12, near)
+
+    def step2(self, i):
+        it, b, s, w = self.views(i)
+        rd, nx, ny = b.rd, self.h.nx, self.h.ny
+        self.m_dx(i).wait_recv()
+        tiles(2, lambda j: self.add(i, ny, j, rd.at[s, 0, j, :, 0:w]))
+        self.go(i, self.m_y(i))
+        self.m_dy(i).wait_recv()
+        tiles(2, lambda j: self.add(i, nx, 2 + j, rd.at[s, 1, j, :, 0:w]))
+        self.go(i, self.m_x(i))
+
+    def step3(self, i):
+        it, b, s, w = self.views(i)
+        rxy, dp = b.rxy, self.h.dp
+        self.m_x(i).wait_recv()
+        self.m_y(i).wait_recv()
+        tiles(4, lambda j: self.add(i, dp, j, rxy.at[s, 0, j, :, 0:w], rxy.at[s, 1, j, :, 0:w]))
+        self.go(i, *[self.m_z(i, k) for k in range(3)])
+
+    def step4(self, i):
+        it, b, s, w = self.views(i)
+        rz = b.rz
+        for k in range(3):
+            self.m_z(i, k).wait_recv()
+        total = self.mine(i, self.h.dp, self.h.z)[...].astype(f32)
+        for k in range(3):
+            total = total + rz[s, k, :, 0:w].astype(f32)
+        it.out[:, pl.ds(it.c0, w)] = total
+        if it.reused:
+            for k, d in enumerate(self.h.peers):
+                pl.semaphore_signal(
+                    self.free.at[it.cls, k if k < 3 else 8 - k], inc=1, device_id=d, device_id_type=MESH
+                )
+
+    def finish(self):
+        for i in list(self.sends):
+            self.release(i)
+
+
+def scatter_plan(specs, ring):
+    items, by_class = [], {}
+    for m, c0, w, cls in specs:
+        mine = by_class.setdefault(cls, [])
+        it = SimpleNamespace(m=m, c0=c0, w=w, cls=cls, slot=len(mine) % ring[cls], before=None, reused=False)
+        if len(mine) >= ring[cls]:
+            it.before = mine[-ring[cls]]
+            items[it.before].reused = True
+        mine.append(len(items))
+        items.append(it)
+    return items
+
+
+def scatter_scratch(held, slots, r, w, dt):
+    return dict(
+        g=pltpu.VMEM((slots, 4, 4, 2, r, w) if held else (8, 128), dt),
+        p=pltpu.VMEM((8, 128) if held else (slots, 4, 4, r, w), dt),
+        r1=pltpu.VMEM((slots, 4, 4, r, w), dt),
+        rd=pltpu.VMEM((slots, 2, 2, r, w), dt),
+        rxy=pltpu.VMEM((slots, 2, 4, r, w), dt),
+        rz=pltpu.VMEM((slots, 3, r, w), dt),
+    )
+
+
+BACKWARD_COPIES = 64
+
+
+def backward_kernel(items, trees, *refs):
+    ref = bind(trees, refs)
+    rows, width = ref.cotangent.shape
+    ff = ref.full[FIRST].shape[1]
+    parts = column_parts(ff, width)
+    page = [ref.page.at[i] for i in range(12)]
+    acc, other = ref.wide.at[0], ref.wide.at[1]
+    here = Place()
+    here.barrier()
+    bufs = [SimpleNamespace(**b) for b in ref.rings]
+    bufs[DOWN_RING].g = bufs[IN_RING].p = bufs[GAIN_RING].p = None
+    items = [SimpleNamespace(**vars(it), out=ref.grads[it.m], src=ref.down_partial) for it in items]
+    rs = Scatter(here, items, bufs, ref.ssem, ref.rsem, ref.lsem, ref.free)
+    cp = Saves(ref.csem)
+    size, half_rows = 128, rows // 2
+    live_len = ref.lengths[0]
+    index = {(it.m, it.c0): i for i, it in enumerate(items)}
+
+    def live(first, n):
+        return lax.broadcasted_iota(jnp.int32, (n, 1), 0) + first < live_len
+
+    def load(n, src, c0=None, w=None, by_row=False):
+        dst = page[n]
+        if c0 is not None:
+            if by_row:
+                src, dst = src.at[pl.ds(c0, w)], dst.at[pl.ds(0, w)]
+            else:
+                src, dst = src.at[:, pl.ds(c0, w)], dst.at[:, pl.ds(0, w)]
+        cp.start(n, src, dst)
+
+    def halves(f):
+        return [functools.partial(f, pl.ds(half_rows * n, half_rows)) for n in range(2)]
+
+    work = []
+
+    def piece(cost, f, needs=(), gives=None):
+        work.append((f, cost, needs, gives))
+
+    def grad_item(m, c0, w, left, right):
+        i = index[m, c0]
+        it = items[i]
+        g = bufs[it.cls].g
+
+        def half(n):
+            def run():
+                if n == 0:
+                    if it.before is not None:
+                        rs.release(it.before)
+                    left_wait = [k for k in range(12) if page[k] is left or page[k] is right]
+                    cp.wait(*left_wait)
+                cols = slice(n * (width // 2), (n + 1) * (width // 2))
+                got = dot_tn(left[:, cols], right[:, 0:w]).astype(bf16)
+                g[it.slot, 2 * n : 2 * n + 2, :, :, :, 0:w] = got.reshape((2,) + g.shape[2:5] + (w,))
+
+            return run
+
+        needs = () if it.before is None else (it.before,)
+        piece(1.25, half(0), needs)
+        piece(1.25, half(1), (), i)
+
+    load(0, ref.cotangent)
+    load(2, ref.full[DOWN], *parts[0], by_row=True)
+    load(4, ref.save_g2, *parts[0])
+    load(3, ref.save_g1, *parts[0])
+    load(1, ref.save_a2)
+    load(5, ref.full[FIRST], *parts[0])
+    load(6, ref.full[SECOND], *parts[0])
+    load(9, ref.save_h)
+    load(10, ref.full[OUT])
+    load(11, ref.save_gp)
+    cp.start(12, ref.save_inv_in, ref.inv_in)
+    cp.start(13, ref.save_inv_mix, ref.inv_mix)
+    cp.start(14, ref.save_inv_mid, ref.inv_mid)
+    cp.start(15, ref.full_gain, ref.gain)
+
+    def hidden_back(j, n):
+        c0, w = parts[j]
+
+        def run():
+            cp.wait(0, 2, 3, 4)
+            r = pl.ds(half_rows * n, half_rows)
+            de = dot_nt(page[0][r, :], page[2][0:w, :])
+            de = jnp.where(live(half_rows * n, half_rows), de, 0.0)
+            page[7][r, 0:w] = (de * page[4][r, 0:w].astype(f32)).astype(bf16)
+            page[8][r, 0:w] = (de * page[3][r, 0:w].astype(f32)).astype(bf16)
+            if n == 1:
+                if j + 1 < len(parts):
+                    load(2, ref.full[DOWN], *parts[j + 1], by_row=True)
+                    load(3, ref.save_g1, *parts[j + 1])
+                    load(4, ref.save_g2, *parts[j + 1])
+                else:
+                    load(3, ref.save_o)
+
+        return run
+
+    def mid_back(j, n):
+        c0, w = parts[j]
+
+        def run():
+            cp.wait(5, 6)
+            r = pl.ds(half_rows * n, half_rows)
+            part = dot_nt(page[7][r, 0:w], page[5][:, 0:w]) + dot_nt(page[8][r, 0:w], page[6][:, 0:w])
+            acc[r, :] = part if j == 0 else acc[r, :] + part
+            if n == 1:
+                if j + 1 < len(parts):
+                    load(5, ref.full[FIRST], *parts[j + 1])
+                    load(6, ref.full[SECOND], *parts[j + 1])
+                else:
+                    load(6, ref.save_a1)
+                    load(7, ref.save_q)
+                    load(8, ref.save_k)
+
+        return run
+
+    for j, (c0, w) in enumerate(parts):
+        for n in range(2):
+            piece(1.7, hidden_back(j, n))
+        grad_item(FIRST, c0, w, page[1], page[7])
+        grad_item(SECOND, c0, w, page[1], page[8])
+        for n in range(2):
+            piece(2.6, mid_back(j, n))
+
+    def middle_back():
+        cp.wait(14, 1, 0)
+
+        def tile(i):
+            r = rows_of(i, size)
+            up, n2 = acc[r, :], page[1][r, :].astype(f32)
+            mean = jnp.mean(up * n2, axis=-1, keepdims=True)
+            dy = page[0][r, :].astype(f32) + ref.inv_mid[r, 0:1] * (up - n2 * mean)
+            acc[r, :] = dy
+            page[2][r, :] = jnp.where(live(i * size, size), dy, 0.0).astype(bf16)
+
+        tiles(rows // size, tile)
+        load(0, ref.full[GATE])
+
+    piece(3.0, middle_back)
+    grad_item(OUT, 0, width, page[9], page[2])
+
+    def branch_back():
+        cp.wait(10)
+
+        def tile(i):
+            r = rows_of(i, half_rows)
+            other[r, :] = dot_nt(page[2][r, :], page[10][...])
+
+        tiles(2, tile)
+        load(9, ref.save_v)
+        load(10, ref.save_pb)
+
+    piece(2.4, branch_back)
+
+    def mix_back(first, count):
+        def run():
+            cp.wait(15, 13, 3, 11)
+            gains = ref.gain
+            gain = jnp.concatenate(
+                [
+                    sum(gains[g, j, cc, 0:1, :].astype(f32) for j in (2 * half, 2 * half + 1) for cc in range(2))
+                    for g in range(4)
+                    for half in range(2)
+                ],
+                axis=1,
+            )
+            terms = ref.gain_terms
+            if first == 0:
+                terms[...] = jnp.zeros_like(terms)
+
+            def tile(i):
+                r = rows_of(i + first, size)
+                inv = ref.inv_mix[r, 0:1]
+                up, z = other[r, :], page[11][r, :].astype(f32)
+                normed = page[3][r, :].astype(f32) * inv
+                sig = jax.nn.sigmoid(z)
+                upu = up * (z * sig)
+                terms[...] += (upu * normed).reshape(size // 8, 8, width).sum(axis=0)
+                page[4][r, :] = (up * normed * gain * sig * (1.0 + z * (1.0 - sig))).astype(bf16)
+                dm = upu * gain
+                mean = jnp.mean(dm * normed, axis=-1, keepdims=True)
+                page[5][r, :] = (inv * (dm - normed * mean)).astype(bf16)
+
+            tiles(count, tile)
+
+        return run
+
+    for n in range(2):
+        piece(3.0, mix_back(n * (rows // size // 2), rows // size // 2))
+
+    def gain_item():
+        g, terms = bufs[GAIN_RING].g, ref.gain_terms
+        for yx in range(4):
+            for z in range(4):
+                for c in range(2):
+                    at = 128 * (2 * yx + z // 2)
+                    g[0, yx, z, c] = terms[:, at : at + 128]
+
+    piece(0.3, gain_item, (), index[GAIN, 0])
+    grad_item(GATE, 0, width, page[6], page[4])
+
+    def attention_back(n, count):
+        def run():
+            cp.wait(7, 8, 9, 10)
+            q, k, v, pb, do, dq, dk, dv = [page[m] for m in (7, 8, 9, 10, 5, 11, 3, 2)]
+            tiles(count, lambda b: attend_blocks_back(b + n * count, q, k, v, pb, do, dq, dk, dv))
+            if n == rows // BLOCK // 4 - 1:
+                load(7, ref.full[QUERY])
+                load(8, ref.full[KEY])
+                load(9, ref.full[VALUE])
+                load(10, ref.save_e, *parts[0])
+                load(5, ref.save_e, *parts[1])
+                load(1, ref.save_e, *parts[2])
+
+        return run
+
+    for n in range(rows // BLOCK // 4):
+        piece(2.4, attention_back(n, 2))
+    grad_item(QUERY, 0, width, page[6], page[11])
+    grad_item(KEY, 0, width, page[6], page[3])
+    grad_item(VALUE, 0, width, page[6], page[2])
+
+    def input_part(up, w, first, then=None):
+        def run():
+            cp.wait(w)
+
+            def tile(i):
+                r = rows_of(i, half_rows)
+                part = dot_nt(page[up][r, :], page[w][...])
+                other[r, :] = part if first else other[r, :] + part
+
+            tiles(2, tile)
+            if then is not None:
+                load(w, ref.full[DOWN], *parts[then], by_row=True)
+
+        return run
+
+    piece(2.4, input_part(4, 0, True))
+    for then, (up, w) in enumerate(((11, 7), (3, 8), (2, 9))):
+        piece(2.4, input_part(up, w, False, then))
+
+    def input_back():
+        cp.wait(12, 6)
+
+        def tile(i):
+            r = rows_of(i, size)
+            up, n1 = other[r, :], page[6][r, :].astype(f32)
+            mean = jnp.mean(up * n1, axis=-1, keepdims=True)
+            page[0][r, :] = (acc[r, :] + ref.inv_in[r, 0:1] * (up - n1 * mean)).astype(bf16)
+
+        tiles(rows // size, tile)
+        cp.start(0, page[0], ref.input_grad)
+        cp.start(16, ref.save_y, acc)
+
+    piece(2.5, input_back)
+
+    def output_part(j, e, w):
+        def run():
+            cp.wait(e, w)
+            n = parts[j][1]
+
+            def tile(i):
+                r = rows_of(i, half_rows)
+                part = dot_nn(page[e][r, 0:n], page[w][0:n, :])
+                other[r, :] = part if j == 0 else other[r, :] + part
+
+            tiles(2, tile)
+
+        return run
+
+    for j, (e, w) in enumerate(((10, 7), (5, 8), (1, 9))):
+        piece(2.4, output_part(j, e, w))
+
+    def output():
+        cp.wait(16)
+
+        def tile(i):
+            r = rows_of(i, size)
+            page[4][r, :] = (acc[r, :] + jnp.where(live(i * size, size), other[r, :], 0.0)).astype(bf16)
+
+        tiles(rows // size, tile)
+        cp.start(4, page[4], ref.layer_out)
+
+    piece(1.5, output)
+
+    def unit(i):
+        it = items[i]
+        return it.w * it.out.shape[0] / (32 * 1024)
+
+    steps = []
+    for i in range(len(items)):
+        u = unit(i)
+        steps.append([
+            (rs.step0, -i - 1, 1.5 * u, 0.2), (rs.step1, 1, 2.8 * u, 1.0 * u + 0.2),
+            (rs.step2, 1, 5.6 * u, 0.4 * u + 0.2), (rs.step3, 2, 5.6 * u, 0.4 * u + 0.2),
+            (rs.step4, None, 0.0, 0.2 * u + 0.2),
+        ])
+    given = [i for i, it in enumerate(items) if it.cls == DOWN_RING]
+    after = [set() if it.before is None else {it.before} for it in items]
+    order = Timeline(steps, work, 3, given, after)
+    order.run()
+    rs.finish()
+    cp.finish()
+    if SHOW_ORDER:
+        print(order.log)
+
+
+SHOW_ORDER = False
+
+
+DOWN_RING, IN_RING, GAIN_RING = range(3)
+
+
+def backward(cotangent, lengths, full, got):
+    rows, width = cotangent.shape
+    flat = [w.reshape(-1, w.shape[-1]) for w in full]
+    ff = flat[FIRST].shape[1]
+    r_in, r_down = full[QUERY].shape[3], full[DOWN].shape[3]
+    parts = column_parts(ff, width)
+    specs = [(DOWN, c0, w, DOWN_RING) for c0, w in column_parts(width, 256)]
+    specs += [(m, c0, w, IN_RING) for c0, w in parts for m in (FIRST, SECOND)]
+    specs += [(OUT, 0, width, IN_RING), (GAIN, 0, 128, GAIN_RING)]
+    specs += [(m, 0, width, IN_RING) for m in (GATE, QUERY, KEY, VALUE)]
+    slots = (2, 4, 1)
+    items = scatter_plan(specs, slots)
+    n = len(items)
+    ins = dict(cotangent=cotangent, full=flat, full_gain=full[GAIN])
+    ins |= {k: a for k, a in got.items() if k != DOWN_PARTIAL}
+    ins |= dict(down_partial=got[DOWN_PARTIAL].reshape(full[DOWN].shape))
+    shapes = [(r_down if m == DOWN else r_in, flat[m].shape[1]) for m in range(len(full))]
+    shapes[GAIN] = (8, 128)
+    page = jax.ShapeDtypeStruct((rows, width), bf16)
+    outs = dict(layer_out=page, input_grad=page)
+    grads = dict(grads=[jax.ShapeDtypeStruct(s, f32) for s in shapes])
+    inv = pltpu.VMEM((rows, 128), f32)
+    scratch = dict(
+        rings=[
+            scatter_scratch(False, slots[DOWN_RING], r_down, 256, bf16),
+            scatter_scratch(True, slots[IN_RING], r_in, width, bf16),
+            scatter_scratch(True, slots[GAIN_RING], 8, 128, f32),
+        ],
+        page=pltpu.VMEM((12, rows, width), bf16),
+        wide=pltpu.VMEM((2, rows, width), f32),
+        inv_in=inv, inv_mix=inv, inv_mid=inv,
+        gain=pltpu.VMEM(full[GAIN].shape, bf16),
+        gain_terms=pltpu.VMEM((8, width), f32),
+        ssem=pltpu.SemaphoreType.DMA((n, 8)),
+        rsem=pltpu.SemaphoreType.DMA((n, 8)),
+        lsem=pltpu.SemaphoreType.DMA((n,)),
+        csem=pltpu.SemaphoreType.DMA((BACKWARD_COPIES,)),
+        free=pltpu.SemaphoreType.REGULAR((len(slots), 6)),
+    )
+    hbm, vmem = pl.BlockSpec(memory_space=pl.ANY), pl.BlockSpec(memory_space=pltpu.VMEM)
+    leaves = jax.tree.leaves
+    out = pl.pallas_call(
+        functools.partial(backward_kernel, items, (dict(lengths=0), ins, outs, grads, scratch)),
+        out_shape=leaves(outs) + leaves(grads),
+        in_specs=[pl.BlockSpec(memory_space=pltpu.SMEM)] + [hbm] * len(leaves(ins)),
+        out_specs=[hbm] * len(leaves(outs)) + [vmem] * len(leaves(grads)),
+        scratch_shapes=leaves(scratch),
+        compiler_params=pltpu.CompilerParams(
+            collective_id=1, has_side_effects=True, vmem_limit_bytes=63 * 2**20
+        ),
+    )(lengths, *leaves(ins))
+    return bind((outs, grads), out)
+
+
+def slice_body(
+    tokens, lengths, cotangent, w_query, w_key, w_value, w_gate, w_out, out_gain, w_first, w_second, w_down,
+):
+    rows, width = tokens.shape[0] * tokens.shape[1], tokens.shape[2]
+    me = lax.axis_index(AXES[0]) * 8 + lax.axis_index(AXES[1])
+    lane = lax.broadcasted_iota(jnp.int32, (16, 128), 1)
+    gain_block = jnp.where(lax.div(lane, 32) == lax.rem(me, 4), jnp.tile(out_gain, 4)[None, :], 0)
+    flat_cotangent = cotangent.reshape(rows, width)
+    shards = (w_query, w_key, w_value, w_gate, gain_block, w_out, w_first, w_second, w_down)
+    full, got = forward(tokens.reshape(rows, width), lengths, flat_cotangent, shards)
+    back = backward(flat_cotangent, lengths, full, got)
+    grads = back.grads
+    gain = lax.dynamic_slice(grads[GAIN].sum(axis=0), (lax.rem(me, 4) * 32,), (32,))
+    return (
+        back.layer_out.reshape(tokens.shape), back.input_grad.reshape(tokens.shape),
+        *[grads[m] for m in (QUERY, KEY, VALUE, GATE, OUT)], gain,
+        *[grads[m] for m in (FIRST, SECOND, DOWN)],
+    )
+
+
 def solution(mesh):
+    fits = (mesh.shape[AXES[0]], mesh.shape[AXES[1]]) == (4, 8)
     return jax.shard_map(
-        body,
+        slice_body if fits else general_body,
         mesh=mesh,
         in_specs=(
-            P(("dp", "fsdp"), None, None),
-            P(("dp", "fsdp")),
-            P(("dp", "fsdp"), None, None),
-            P(("dp", "fsdp"), None),
-            P(("dp", "fsdp"), None),
-            P(("dp", "fsdp"), None),
-            P(("dp", "fsdp"), None),
-            P(("dp", "fsdp"), None),
-            P(("dp", "fsdp")),
-            P(("dp", "fsdp"), None),
-            P(("dp", "fsdp"), None),
-            P(("dp", "fsdp"), None),
+            P(AXES, None, None),
+            P(AXES),
+            P(AXES, None, None),
+            P(AXES, None),
+            P(AXES, None),
+            P(AXES, None),
+            P(AXES, None),
+            P(AXES, None),
+            P(AXES),
+            P(AXES, None),
+            P(AXES, None),
+            P(AXES, None),
         ),
         out_specs=(
-            P(("dp", "fsdp"), None, None),
-            P(("dp", "fsdp"), None, None),
-            P(("dp", "fsdp"), None),
-            P(("dp", "fsdp"), None),
-            P(("dp", "fsdp"), None),
-            P(("dp", "fsdp"), None),
-            P(("dp", "fsdp"), None),
-            P(("dp", "fsdp")),
-            P(("dp", "fsdp"), None),
-            P(("dp", "fsdp"), None),
-            P(("dp", "fsdp"), None),
+            P(AXES, None, None),
+            P(AXES, None, None),
+            P(AXES, None),
+            P(AXES, None),
+            P(AXES, None),
+            P(AXES, None),
+            P(AXES, None),
+            P(AXES),
+            P(AXES, None),
+            P(AXES, None),
+            P(AXES, None),
         ),
         check_vma=False,
     )

time: 1350 us -> 333 us (0.25)
  waiting for transfers between devices: 897 us -> 0 us
  Pallas kernels: 0 us -> 312 us
  matrix products: 214 us -> 0 us
  local copies, waits for them, and re-layouts: 137 us -> 11.4 us
  blocking collectives: 42.2 us -> 0 us
  other arithmetic: 33.7 us -> 1.31 us
    reduce_scatter x3 -> x0, waiting for transfers between devices: 572 us -> none  [the longest x1 248 us: ffn_sums(): lax.psum_scatter(weight_grad(second_in, both_proj), ('dp', 'fsdp'), scatt...]
    all_gather x8 -> x0, waiting for transfers between devices: 320 us -> none  [the longest x1 61.3 us: body(): lax.all_gather(w_second, ('dp', 'fsdp'), axis=0, tiled=True)]
    pallas_call x0 -> x2, Pallas kernels: none -> 312 us  [the longest x1 166 us: backward(): pl.pallas_call(functools.partial(backward_kernel, items, (dict(lengths=0)...]
    dot_general x26 -> x0, matrix products: 214 us -> none  [the longest x8 64.9 us: project(): return jnp.dot(left_rows, right_rows, preferred_element_type=jnp.float32)]
    reshape x8 -> x0, local copies, waits for them, and re-layouts: 59 us -> none  [the longest x6 38.1 us: split_heads(): return row_block.reshape(row_count // BLOCK, BLOCK, HEADS, HEAD_DIM)]
    convert_element_type x8 -> x0, local copies, waits for them, and re-layouts: 50.7 us -> none  [the longest x3 18.3 us: attend_back(): grad_keys.reshape(row_count, -1).astype(jnp.bfloat16)]
    unnamed x1 -> x0, blocking collectives: 42.2 us -> none
    concatenate x1 -> x0, other arithmetic: 15.7 us -> none  [body(): jnp.concatenate([from_input, from_branch, gain_part], axis=1)]
  transfers between devices with their start and end apart: 11 -> 0, of which waited for: 11 -> 0; matrix products, arithmetic and copies ran while one was open for 15% -> 0% of each run, Pallas kernels for 0% -> 0%
where the time goes in v2:
time: 333 us; the launch traced here: 326 us
  Pallas kernels  312 us (94%)
  local copies, waits for them, and re-layouts  11.4 us (3%)
    pallas_call x1, Pallas kernels, backward(): pl.pallas_call(functools.partial(backward_kernel, items, (dict(lengths=0)...  166 us
    pallas_call x1, Pallas kernels, forward(): pl.pallas_call(functools.partial(forward_kernel, items, (dict(lengths=0),...  145 us
    unnamed x28, local copies, waits for them, and re-layouts  10.1 us

profile of v2, /device:TPU:0, one launch (start us, length us, event | category | flops | bytes accessed | tf_op | source)
XLA Modules:
  0.0 326.4 jit_solution(6001614011812883959)
XLA Ops:
  1.3 0.7 tile.2
  2.0 0.1 broadcast_in_dim.14
  2.1 0.6 broadcast_select_fusion.refs_6_
  2.7 145.4 %shard_map.203 = (bf16[4,4,2,32,1024]{4,3,2,1,0:T(8,128)(2,1)}, bf16[4,4,2,32,1024]{4,3,2,1,0:T(8,128)(2,1)}, bf16[4,4,2,32,1024]{4,3,2,1,0:T(8,128)(2,1)}, bf16...) custom-call(s32[1]{0:T(128)S(6)} %copy.33.refs_0_, ...), custom_call_target="tpu_custom_call" | custom-call | tf_op jit(solution)/shard_map/pallas_call | solution.py:762
  148.1 166.5 %shard_map.204 = (bf16[1024,1024]{1,0:T(8,128)(2,1)}, bf16[1024,1024]{1,0:T(8,128)(2,1)}, f32[32,1024]{1,0:T(8,128)}, f32[32,1024]{1,0:T(8,128)}, f32[32,1024]{1...) custom-call(s32[1]{0:T(128)S(6)} %copy.33.refs_0_, ...), custom_call_target="tpu_custom_call" | custom-call | tf_op jit(solution)/shard_map/pallas_call | solution.py:1346
  314.6 0.7 reduce_sum.9
  315.3 0.6 dynamic_slice.3
  315.9 0.0 copy-start
  315.9 3.2 copy.34
  319.1 0.0 copy-done
  319.1 0.0 copy-start.8
  319.1 0.0 copy-start.7
  319.1 0.0 copy-start.6
  319.1 0.0 copy-start.5
  319.1 0.0 copy-start.4
  319.1 0.0 copy-start.3
  319.1 0.0 copy-start.2
  319.1 1.3 copy.35
  320.5 0.0 copy-done.8
  320.5 0.0 copy-start.1
  320.5 0.7 copy.36
  321.1 0.0 copy-done.7
  321.1 0.7 copy.37
  321.8 0.0 copy-done.6
  321.8 0.7 copy.38
  322.4 0.0 copy-done.5
  322.4 0.7 copy.39
  323.1 0.0 copy-done.4
  323.1 0.7 copy.40
  323.8 0.0 copy-done.3
  323.8 0.7 copy.41
  324.5 0.0 copy-done.2
  324.5 0.7 copy.42
  325.2 0.0 copy-done.1
  325.2 0.7 copy.43
  (1 shorter events, 0.0 us)
Async XLA Ops:
  315.9 3.2 copy-start
  319.1 1.4 copy-start.8
  319.1 2.0 copy-start.7
  319.1 2.7 copy-start.6
  319.1 3.3 %copy-start.5 = (f32[32,1024]{1,0:T(8,128)S(1)}, f32[32,1024]{1,0:T(8,128)}, u32[]{:S(2)}) copy-start(f32[32,1024]{1,0:T(8,128)} %get-tuple-element.101) | copy-start | bytes 393220
  319.1 4.0 %copy-start.4 = (f32[32,1024]{1,0:T(8,128)S(1)}, f32[32,1024]{1,0:T(8,128)}, u32[]{:S(2)}) copy-start(f32[32,1024]{1,0:T(8,128)} %get-tuple-element.102) | copy-start | bytes 393220
  319.1 4.6 %copy-start.3 = (f32[32,2816]{1,0:T(8,128)S(1)}, f32[32,2816]{1,0:T(8,128)}, u32[]{:S(2)}) copy-start(f32[32,2816]{1,0:T(8,128)} %get-tuple-element.104) | copy-start | bytes 1081348
  319.1 5.4 %copy-start.2 = (f32[32,2816]{1,0:T(8,128)S(1)}, f32[32,2816]{1,0:T(8,128)}, u32[]{:S(2)}) copy-start(f32[32,2816]{1,0:T(8,128)} %get-tuple-element.105) | copy-start | bytes 1081348
  320.5 4.8 %copy-start.1 = (f32[88,1024]{1,0:T(8,128)S(1)}, f32[88,1024]{1,0:T(8,128)}, u32[]{:S(2)}) copy-start(f32[88,1024]{1,0:T(8,128)} %get-tuple-element.106) | copy-start | bytes 1081348
